TPU v7x, 32 devices: a whole 2x2x4 slice. The times are simulated.
32 devices in a mesh: parts: 2 (over y), tensor: 4 (over x, core), dp: 4 (over z).
Axes of the slice: x: 2, y: 2, z: 4, core: 2. Of those that a mesh axis runs over, the one named last changes fastest.
Arguments:
- hidden: bfloat16 [2048, 53248], P(('parts', 'dp'), 'tensor'), parts along dimension 0, may hold values from -6 to 6
- down_weight: bfloat16 [53248, 512], P('tensor'), may hold values from -0.02734375 to 0.02734375
- cotangent: bfloat16 [2048, 512], P(('parts', 'dp')), parts along dimension 0, may hold values from -64 to 64
Outputs:
- output: bfloat16 [2048, 512], P(('parts', 'dp')), parts along dimension 0
- weight_grad: bfloat16 [106496, 512], P(('parts', 'tensor')), parts along dimension 0
- hidden_grad: bfloat16 [2048, 53248], P(('parts', 'dp'), 'tensor'), parts along dimension 0
There are 2 independent parts, one for each index of `parts`. A program takes and returns all parts, laid end to end along the dimension named above; an argument that names none is the same for every part. Nothing has to cross between parts.
All inputs are finite; a program needn't handle non-finite values.
Results may differ from a plain program's by a relative error of at most 0.0051.
Values may be sent and summed in bfloat16 or wider, within the bound.
No kernel may reach another device: no remote copies, remote signals or barrier semaphores. Data moves between devices by JAX's collectives and lax.ppermute only.
A program may use at most 192 MiB of HBM per device.

v0:
```python
import math

import jax
import jax.numpy as jnp
from jax import lax
from jax.sharding import PartitionSpec as P

HAD = 4096
GROUPS = 13


def swapped(shard, axis, stride):
    return lax.ppermute(shard, axis, [(i, i ^ 1 << stride) for i in range(lax.axis_size(axis))])


def sign_table(order_size, kind):
    indices = jnp.arange(order_size, dtype=jnp.int32)
    intersection = jnp.bitwise_and(indices[:, None], indices[None, :])
    parity_count = jnp.zeros((order_size, order_size), jnp.int32)
    for bit_pos in range(order_size.bit_length() - 1):
        parity_count = parity_count + jnp.bitwise_and(jnp.right_shift(intersection, bit_pos), 1)
    return (1 - 2 * jnp.bitwise_and(parity_count, 1)).astype(kind)


def rotate(values):
    row_count = values.shape[0]
    local_size = values.shape[1] // GROUPS
    scale_factor = 1.0 / math.sqrt(HAD)
    blocks = values.reshape(row_count, GROUPS, local_size)
    current = jnp.einsum(
        "rcq,qs->rcs",
        blocks,
        sign_table(local_size, jnp.bfloat16),
        preferred_element_type=jnp.float32,
    )
    position = lax.axis_index("tensor")
    sections = lax.axis_size("tensor").bit_length() - 1
    for bit_pos in range(sections):
        partner = swapped(current, "tensor", bit_pos)
        upper_half = jnp.bitwise_and(jnp.right_shift(position, bit_pos), 1) == 1
        current = jnp.where(upper_half, partner - current, current + partner)
    return (current * scale_factor).reshape(row_count, -1).astype(jnp.bfloat16)


def local(hidden, down_weight, cotangent):
    rotated = rotate(hidden)
    part_out = jnp.dot(rotated, down_weight, preferred_element_type=jnp.float32)
    output = lax.psum(part_out, "tensor").astype(jnp.bfloat16)
    token_total = cotangent.shape[0] * lax.axis_size("dp")
    part_grad = lax.dot_general(
        rotated, cotangent, (((0,), (0,)), ((), ())), preferred_element_type=jnp.float32
    )
    local_share = (
        lax.psum_scatter(part_grad, "dp", scatter_dimension=0, tiled=True) / token_total
    ).astype(jnp.bfloat16)
    weight_grad = lax.all_gather(local_share, "dp", axis=0, tiled=True)
    back_grad = lax.dot_general(
        cotangent, down_weight, (((1,), (1,)), ((), ())), preferred_element_type=jnp.float32
    ).astype(jnp.bfloat16)
    hidden_grad = rotate(back_grad)
    return (output, weight_grad, hidden_grad)


def solution(mesh):
    return jax.shard_map(
        local,
        mesh=mesh,
        in_specs=(P(("parts", "dp"), "tensor"), P("tensor", None), P(("parts", "dp"), None)),
        out_specs=(
            P(("parts", "dp"), None),
            P(("parts", "tensor"), None),
            P(("parts", "dp"), "tensor"),
        ),
        check_vma=False,
    )
```

profile of v0, /device:TPU:0, one launch (start us, length us, event | category | flops | bytes accessed | tf_op | source)
XLA Modules:
  0.0 1207.2 jit_solution(3541217287139696712)
XLA Ops:
  7.2 9.9 copy.13
  17.2 17.3 %convolution_bitcast_fusion = f32[256,13,1024]{0,2,1:T(8,128)} fusion(bf16[256,13,1024]{0,2,1:T(8,128)(2,1)} %bitcast.23), kind=kOutput, calls=%fused_computation.5 | convolution fusion | flops 7014973440 | bytes 20447232 | tf_op jit(solution)/shard_map/rcq,qs->rcs/dot_general | solution.py:30
  34.4 0.5 collective-permute-start
  34.9 20.6 %collective-permute-done = f32[256,13,1024]{0,2,1:T(8,128)} collective-permute-done((f32[256,13,1024]{0,2,1:T(8,128)}, f32[256,13,1024]{0,2,1:T(8,128)}, u32[]{:S(2)}, u32[]{:S(2)}) %collective-permute-start) | collective-permute-done | bytes 13631520 | tf_op jit(solution)/shard_map/ppermute | solution.py:13
  55.5 14.5 %add_select_fusion.1 = f32[256,13,1024]{0,2,1:T(8,128)} fusion(f32[256,13,1024]{0,2,1:T(8,128)} %convolution_bitcast_fusion, f32[256,13,1024]{0,2,1:T(8,128)} %collective-permute-done, pred[]{:T(512)S(6)} %eq.9), kind=kLoop, calls=%fused_computation.4 | loop fusion | flops 10223616 | bytes 40894464 | tf_op jit(solution)/shard_map/jit(_where)/select_n | solution.py:41
  70.0 2.9 collective-permute-start.1
  72.9 293.4 %collective-permute-done.1 = f32[256,13,1024]{0,2,1:T(8,128)} collective-permute-done((f32[256,13,1024]{0,2,1:T(8,128)}, f32[256,13,1024]{0,2,1:T(8,128)}, u32[]{:S(2)}, u32[]{:S(2)}) %collective-permute-start.1) | collective-permute-done | bytes 13631520 | tf_op jit(solution)/shard_map/ppermute | solution.py:13
  366.3 9.7 multiply_convert_fusion.1
  376.0 2.8 copy-done.2
  378.9 10.9 fusion.31
  389.8 0.2 all-gather.2.cloned.1.call-start
  390.0 15.6 %convolution_convert_fusion = bf16[256,13312]{1,0:T(8,128)(2,1)} fusion(bf16[256,512]{1,0:T(8,128)(2,1)S(1)} %copy-done, bf16[13312,512]{1,0:T(8,128)(2,1)} %param.4), kind=kOutput, calls=%fused_computation | convolution fusion | flops 3493068800 | bytes 20709376 | tf_op jit(solution)/shard_map/dot_general | solution.py:57
  405.7 9.9 copy.16
  415.6 17.0 %fusion.1 = f32[256,13,1024]{0,2,1:T(8,128)} fusion(bf16[256,13,1024]{0,2,1:T(8,128)(2,1)} %bitcast.22), kind=kOutput, calls=%fused_computation.9 | convolution fusion | flops 7014973440 | bytes 20447232 | tf_op jit(solution)/shard_map/rcq,qs->rcs/dot_general | solution.py:30
  432.7 406.7 %reduce-scatter.2.cloned.1.call-done = f32[3328,512]{1,0:T(8,128)} async-done(((f32[13312,512]{1,0:T(8,128)}), f32[3328,512]{1,0:T(8,128)}) %reduce-scatter.2.cloned.1.call-update) | async-done | bytes 6815760 | tf_op jit(solution)/shard_map/reduce_scatter | solution.py:54
  839.3 5.6 multiply_convert_fusion.2
  845.0 9.8 add_select_fusion
  854.8 1.6 collective-permute-start.3
  856.4 293.1 %collective-permute-done.3 = f32[256,13,1024]{0,2,1:T(8,128)S(1)} collective-permute-done((f32[256,13,1024]{0,2,1:T(8,128)S(1)}, f32[256,13,1024]{0,2,1:T(8,128)S(1)}, u32[]{:S(2)}, u32[]{:S(2)}) %collective-permute-start.3) | collective-permute-done | bytes 13631520 | tf_op jit(solution)/shard_map/ppermute | solution.py:13
  1149.5 4.6 multiply_convert_fusion
  1154.1 9.9 copy.21
  1164.1 8.8 fusion.30
  1172.9 17.1 %all-reduce.1 = bf16[256,512]{1,0:T(8,128)(2,1)} all-reduce(f32[256,512]{1,0:T(8,128)S(1)} %fusion.30), channel_id=1, replica_groups=mesh['parts'=2,'tensor'=4,'dp'=4] {'tensor'}, use_global_device_ids=true, to_apply=%region_0.1 | all-reduce | flops 131072 | bytes 786432 | tf_op jit(solution)/shard_map/psum | solution.py:48
  1190.0 10.4 copy.30
  (11 shorter events, 0.1 us)
Async XLA Ops:
  7.2 371.7 %copy-start = (bf16[256,512]{1,0:T(8,128)(2,1)S(1)}, bf16[256,512]{1,0:T(8,128)(2,1)}, u32[]{:S(2)}) copy-start(bf16[256,512]{1,0:T(8,128)(2,1)} %param.5) | copy-start | bytes 786436
  7.2 832.2 %reduce-scatter.2.cloned.1.call-start = ((), (), s32[]{:S(2)}) async-start(), calls=%async_computation.1 | async-start | bytes 34078720 | tf_op jit(solution)/shard_map/reduce_scatter | solution.py:54
  34.4 21.1 %collective-permute-start = (f32[256,13,1024]{0,2,1:T(8,128)}, f32[256,13,1024]{0,2,1:T(8,128)}, u32[]{:S(2)}, u32[]{:S(2)}) collective-permute-start(f32[256,13,1024]{0,2,1:T(8,128)} %convolution_bitcast_fusion), channel_id=1, source_target_pairs={{0,4},{4,0},{8,12},{12,8},{1,5},{5,1},{9,13},{13,9},{2,6},{6,2},{1... | collective-permute-start | bytes 40894472 | tf_op jit(solution)/shard_map/ppermute | solution.py:13
  70.0 296.3 %collective-permute-start.1 = (f32[256,13,1024]{0,2,1:T(8,128)}, f32[256,13,1024]{0,2,1:T(8,128)}, u32[]{:S(2)}, u32[]{:S(2)}) collective-permute-start(f32[256,13,1024]{0,2,1:T(8,128)} %add_select_fusion.1), channel_id=1, source_target_pairs={{0,8},{4,12},{8,0},{12,4},{1,9},{5,13},{9,1},{13,5},{2,10},{6,14},... | collective-permute-start | bytes 40894472 | tf_op jit(solution)/shard_map/ppermute | solution.py:13
  376.0 2.8 copy-start.2
  389.8 800.2 %all-gather.2.cloned.1.call-start = ((), (), s32[]{:S(2)}) async-start(), calls=%async_computation.2 | async-start | bytes 17039360 | tf_op jit(solution)/shard_map/all_gather | solution.py:56
  432.7 412.3 %collective-permute-start.2 = (f32[256,13,1024]{0,2,1:T(8,128)}, f32[256,13,1024]{0,2,1:T(8,128)}, u32[]{:S(2)}, u32[]{:S(2)}) collective-permute-start(f32[256,13,1024]{0,2,1:T(8,128)} %fusion.1), channel_id=1, source_target_pairs={{0,4},{4,0},{8,12},{12,8},{1,5},{5,1},{9,13},{13,9},{2,6},{6,2},{1... | collective-permute-start | bytes 40894472 | tf_op jit(solution)/shard_map/ppermute | solution.py:13
  854.8 294.7 %collective-permute-start.3 = (f32[256,13,1024]{0,2,1:T(8,128)S(1)}, f32[256,13,1024]{0,2,1:T(8,128)S(1)}, u32[]{:S(2)}, u32[]{:S(2)}) collective-permute-start(f32[256,13,1024]{0,2,1:T(8,128)S(1)} %add_select_fusion), channel_id=1, source_target_pairs={{0,8},{4,12},{8,0},{12,4},{1,9},{5,13},{9,1},{13,5},{2,10},{6,14},... | collective-permute-start | bytes 40894472 | tf_op jit(solution)/shard_map/ppermute | solution.py:13
  1190.0 10.4 copy-start.1
Sparse Core Ops, SparseCore 0:
  389.9 449.3 reduce-scatter.1
  845.1 237.4 all-gather.1
where the time goes:
time: 1210 us
  waiting for transfers between devices  1010 us (83%)
  matrix products  69.7 us (6%)
  other arithmetic  44.3 us (4%)
  local copies, waits for them, and re-layouts  43 us (4%)
  blocking collectives  17.1 us (1%)
  between operations  14.1 us (1%)
    ppermute x4, waiting for transfers between devices, swapped(): lax.ppermute(shard, axis, [(i, i ^ 1 << stride) for i in range(lax.axis_s...  607 us
    reduce_scatter x1, waiting for transfers between devices, local(): lax.psum_scatter(part_grad, 'dp', scatter_dimension=0, tiled=True)  407 us
    dot_general x2, matrix products, rotate(): jnp.einsum('rcq,qs->rcs', blocks, sign_table(local_size, jnp.bfloat16), p...  34.3 us
    unnamed x9, local copies, waits for them, and re-layouts  33.1 us
    select_n x2, other arithmetic, rotate(): current = jnp.where(upper_half, partner - current, current + partner)  24.4 us
  transfers between devices with their start and end apart: 6, of which 4 were waited for; matrix products, arithmetic and copies ran while one was open for 7% of the time, Pallas kernels for 0%

commit v1 on v0

v1 whole, which is shorter than its diff:
```python
import math

import jax
import jax.numpy as jnp
from jax import lax
from jax.sharding import PartitionSpec as P

HAD = 4096
GROUPS = 13
CHUNKS = (1, 2, 2, 2, 2, 2, 2)
BF = jnp.bfloat16
F32 = jnp.float32


def sign_table(order_size, kind):
    indices = jnp.arange(order_size, dtype=jnp.int32)
    intersection = jnp.bitwise_and(indices[:, None], indices[None, :])
    parity_count = jnp.zeros((order_size, order_size), jnp.int32)
    for bit_pos in range(order_size.bit_length() - 1):
        parity_count = parity_count + jnp.bitwise_and(jnp.right_shift(intersection, bit_pos), 1)
    return (1 - 2 * jnp.bitwise_and(parity_count, 1)).astype(kind)


def across(values):
    size = lax.axis_size("tensor")
    position = lax.axis_index("tensor")
    current = values.astype(F32)
    for bit_pos in reversed(range(size.bit_length() - 1)):
        partner = lax.ppermute(
            current.astype(BF), "tensor", [(i, i ^ 1 << bit_pos) for i in range(size)]
        )
        sign = (1 - 2 * jnp.bitwise_and(jnp.right_shift(position, bit_pos), 1)).astype(F32)
        current = partner.astype(F32) + sign * current
    return current


def rotate(values, table):
    rows, width = values.shape
    size = table.shape[0]
    mixed = (across(values) * (1.0 / math.sqrt(HAD))).astype(BF)
    turned = jnp.einsum(
        "rcq,qs->rcs", mixed.reshape(rows, width // size, size), table,
        preferred_element_type=F32,
    )
    return turned.reshape(rows, width).astype(BF)


def grad_product(rows, cotangent):
    return lax.dot_general(rows, cotangent, (((0,), (0,)), ((), ())), preferred_element_type=F32)


def over_tokens(rotated, cotangent, outer_cotangent, scale):
    count = lax.axis_size("dp")
    place = lax.axis_index("dp")
    last, half = count - 1, count // 2
    partial = grad_product(rotated, cotangent)
    if half > 1:
        outer = lax.ppermute(rotated, "dp", [(0, 1), (last, last - 1)])
        partial = grad_product(
            jnp.concatenate([rotated, outer], 0),
            jnp.concatenate([cotangent, outer_cotangent], 0),
        )
    for step in range(1, half - 1):
        outer = lax.ppermute(
            partial.astype(BF), "dp", [(step, step + 1), (last - step, last - step - 1)]
        )
        partial = partial + outer.astype(F32)
    mine = partial.astype(BF)
    other = lax.ppermute(mine, "dp", [(half - 1, half), (half, half - 1)])
    total = ((mine.astype(F32) + other.astype(F32)) * scale).astype(BF)
    for step in range(half - 1, 0, -1):
        inner = lax.ppermute(total, "dp", [(step, step - 1), (last - step, last - step + 1)])
        total = jnp.where((place == step - 1) | (place == last - step + 1), inner, total)
    return total


def local(hidden, down_weight, cotangent):
    local_size = HAD // lax.axis_size("tensor")
    count = lax.axis_size("dp")
    table = sign_table(local_size, BF)
    scale = 1.0 / (cotangent.shape[0] * count)
    outer_cotangent = cotangent
    if count > 2:
        outer_cotangent = lax.ppermute(
            cotangent, "dp", [(0, 1), (count - 1, count - 2)]
        )
    grads, backs, part_out = [], [], None
    start = 0
    for groups in CHUNKS:
        span = slice(start * local_size, (start + groups) * local_size)
        start += groups
        rotated = rotate(hidden[:, span], table)
        grads.append(over_tokens(rotated, cotangent, outer_cotangent, scale))
        term = jnp.dot(rotated, down_weight[span], preferred_element_type=F32)
        part_out = term if part_out is None else part_out + term
        back = lax.dot_general(
            cotangent, down_weight[span], (((1,), (1,)), ((), ())), preferred_element_type=F32
        ).astype(BF)
        backs.append(rotate(back, table))
    output = lax.psum(part_out, "tensor").astype(BF)
    return (output, jnp.concatenate(grads, 0), jnp.concatenate(backs, 1))


def solution(mesh):
    return jax.shard_map(
        local,
        mesh=mesh,
        in_specs=(P(("parts", "dp"), "tensor"), P("tensor", None), P(("parts", "dp"), None)),
        out_specs=(
            P(("parts", "dp"), None),
            P(("parts", "tensor"), None),
            P(("parts", "dp"), "tensor"),
        ),
        check_vma=False,
    )
```

time: 1210 us -> 859 us (0.71)
  waiting for transfers between devices: 1010 us -> 500 us
  matrix products: 69.7 us -> 158 us
  starting transfers between devices: 5.17 us -> 72.6 us
  between operations: 14.1 us -> 1.66 us
    reduce_scatter x1 -> x0, waiting for transfers between devices: 407 us -> none  [local(): lax.psum_scatter(part_grad, 'dp', scatter_dimension=0, tiled=True)]
    ppermute x4 -> x50, waiting for transfers between devices: 607 us -> 500 us  [the longest x7 260 us: over_tokens(): lax.ppermute(total, 'dp', [(step, step - 1), (last - step, last - step +...]
    dot_general x5 -> x35, matrix products: 69.7 us -> 158 us  [the longest x14 105 us: rotate(): jnp.einsum('rcq,qs->rcs', mixed.reshape(rows, width // size, size), table...]
    ppermute x4 -> x50, starting transfers between devices: 4.91 us -> 72.6 us  [the longest x28 26.3 us: across(): lax.ppermute(current.astype(BF), 'tensor', [(i, i ^ 1 << bit_pos) for i i...]
    select_n x2 -> x0, other arithmetic: 24.4 us -> none  [rotate(): current = jnp.where(upper_half, partner - current, current + partner)]
    convert_element_type x3 -> x24, other arithmetic: 19.9 us -> 36.3 us  [the longest x8 18.8 us: rotate(): mixed = (across(values) * (1.0 / math.sqrt(HAD))).astype(BF)]
    unnamed x9 -> x72, local copies, waits for them, and re-layouts: 33.1 us -> 20 us
  transfers between devices with their start and end apart: 6 -> 50, of which waited for: 4 -> 17; matrix products, arithmetic and copies ran while one was open for 7% -> 29% of each run, Pallas kernels for 0% -> 0%
where the time goes in v1:
time: 859 us; the launch traced here: 848 us
  waiting for transfers between devices  500 us (58%)
  matrix products  158 us (18%)
  starting transfers between devices  72.6 us (8%)
  other arithmetic  50.2 us (6%)
  local copies, waits for them, and re-layouts  47.9 us (6%)
  blocking collectives  17.6 us (2%)
    ppermute x7, waiting for transfers between devices, over_tokens(): lax.ppermute(total, 'dp', [(step, step - 1), (last - step, last - step +...  260 us
    ppermute x28, waiting for transfers between devices, across(): lax.ppermute(current.astype(BF), 'tensor', [(i, i ^ 1 << bit_pos) for i i...  203 us
    dot_general x14, matrix products, rotate(): jnp.einsum('rcq,qs->rcs', mixed.reshape(rows, width // size, size), table...  105 us
    ppermute x7, waiting for transfers between devices, over_tokens(): outer = lax.ppermute(rotated, 'dp', [(0, 1), (last, last - 1)])  37.4 us
    ppermute x28, starting transfers between devices, across(): lax.ppermute(current.astype(BF), 'tensor', [(i, i ^ 1 << bit_pos) for i i...  26.3 us
    ppermute x7, starting transfers between devices, over_tokens(): outer = lax.ppermute(rotated, 'dp', [(0, 1), (last, last - 1)])  24.7 us
    dot_general x7, matrix products, local(): term = jnp.dot(rotated, down_weight[span], preferred_element_type=F32)  21.4 us
    unnamed x72, local copies, waits for them, and re-layouts  20 us
  transfers between devices with their start and end apart: 50, of which 17 were waited for; matrix products, arithmetic and copies ran while one was open for 29% of the time, Pallas kernels for 0%

profile of v1, /device:TPU:0, one launch (start us, length us, event | category | flops | bytes accessed | tf_op | source)
XLA Modules:
  0.0 848.0 jit_solution(2043226536092685395)
XLA Ops:
  29.9 37.8 %collective-permute-done = bf16[256,1024]{1,0:T(8,128)(2,1)S(1)} collective-permute-done((bf16[256,1024]{1,0:T(8,128)(2,1)S(1)}, bf16[256,1024]{1,0:T(8,128)(2,1)S(1)}, u32[]{:S(2)}, u32[]{:S(2)}) %collective-permute-start) | collective-permute-done | bytes 524320 | tf_op jit(solution)/shard_map/ppermute | solution.py:29
  82.6 7.5 fusion.110
  90.1 18.7 %fusion.111 = bf16[256,1024]{1,0:T(8,128)(2,1)} fusion(bf16[256,1024]{1,0:T(8,128)(2,1)S(1)} %collective-permute-done.37, bf16[256,1024]{1,0:T(8,128)(2,1)} %convolution_convert_fusion.13, bf16[256,1024]{1,0:T(8,128)(2,1)} %collective-permute-done.36, f32[]{:T(128)S(6)} %convert_element_type.476, f32[]{:T(128)S(6)} %convert_element_type.472), kind=kOutput, calls=%fused_computation.138 | convolution fusion | flops 575143936 | bytes 2097160 | tf_op jit(solution)/shard_map/rcq,qs->rcs/dot_general | solution.py:41
  116.9 29.6 %collective-permute-done.38 = bf16[256,2048]{1,0:T(8,128)(2,1)} collective-permute-done((bf16[256,2048]{1,0:T(8,128)(2,1)}, bf16[256,2048]{1,0:T(8,128)(2,1)}, u32[]{:S(2)}, u32[]{:S(2)}) %collective-permute-start.38) | collective-permute-done | bytes 1048608 | tf_op jit(solution)/shard_map/ppermute | solution.py:29
  150.5 18.4 %collective-permute-done.40 = bf16[256,2048]{1,0:T(8,128)(2,1)S(1)} collective-permute-done((bf16[256,2048]{1,0:T(8,128)(2,1)}, bf16[256,2048]{1,0:T(8,128)(2,1)S(1)}, u32[]{:S(2)}, u32[]{:S(2)}) %collective-permute-start.40) | collective-permute-done | bytes 1048608 | tf_op jit(solution)/shard_map/ppermute | solution.py:29
  171.3 20.0 %collective-permute-done.42 = bf16[256,2048]{1,0:T(8,128)(2,1)S(1)} collective-permute-done((bf16[256,2048]{1,0:T(8,128)(2,1)S(1)}, bf16[256,2048]{1,0:T(8,128)(2,1)S(1)}, u32[]{:S(2)}, u32[]{:S(2)}) %collective-permute-start.42) | collective-permute-done | bytes 1048608 | tf_op jit(solution)/shard_map/ppermute | solution.py:29
  193.8 20.0 %collective-permute-done.44 = bf16[256,2048]{1,0:T(8,128)(2,1)S(1)} collective-permute-done((bf16[256,2048]{1,0:T(8,128)(2,1)S(1)}, bf16[256,2048]{1,0:T(8,128)(2,1)S(1)}, u32[]{:S(2)}, u32[]{:S(2)}) %collective-permute-start.44) | collective-permute-done | bytes 1048608 | tf_op jit(solution)/shard_map/ppermute | solution.py:29
  216.2 20.0 %collective-permute-done.46 = bf16[256,2048]{1,0:T(8,128)(2,1)S(1)} collective-permute-done((bf16[256,2048]{1,0:T(8,128)(2,1)S(1)}, bf16[256,2048]{1,0:T(8,128)(2,1)S(1)}, u32[]{:S(2)}, u32[]{:S(2)}) %collective-permute-start.46) | collective-permute-done | bytes 1048608 | tf_op jit(solution)/shard_map/ppermute | solution.py:29
  242.3 16.4 %collective-permute-done.48 = bf16[256,2048]{1,0:T(8,128)(2,1)S(1)} collective-permute-done((bf16[256,2048]{1,0:T(8,128)(2,1)S(1)}, bf16[256,2048]{1,0:T(8,128)(2,1)S(1)}, u32[]{:S(2)}, u32[]{:S(2)}) %collective-permute-start.48) | collective-permute-done | bytes 1048608 | tf_op jit(solution)/shard_map/ppermute | solution.py:29
  266.1 15.1 %collective-permute-done.12 = bf16[256,2048]{1,0:T(8,128)(2,1)S(1)} collective-permute-done((bf16[256,2048]{1,0:T(8,128)(2,1)S(1)}, bf16[256,2048]{1,0:T(8,128)(2,1)S(1)}, u32[]{:S(2)}, u32[]{:S(2)}) %collective-permute-start.12) | collective-permute-done | bytes 1048608 | tf_op jit(solution)/shard_map/ppermute | solution.py:29
  281.2 21.6 %collective-permute-done.2 = bf16[256,2048]{1,0:T(8,128)(2,1)S(1)} collective-permute-done((bf16[256,2048]{1,0:T(8,128)(2,1)S(1)}, bf16[256,2048]{1,0:T(8,128)(2,1)S(1)}, u32[]{:S(2)}, u32[]{:S(2)}) %collective-permute-start.2) | collective-permute-done | bytes 1048608 | tf_op jit(solution)/shard_map/ppermute | solution.py:29
  349.3 6.7 fusion.104
  381.3 10.1 %copy.43 = bf16[256,13312]{1,0:T(8,128)(2,1)} copy(bf16[256,13312]{0,1:T(8,128)(2,1)} %constant_dynamic-update-slice_fusion.2) | data formatting | bytes 13631488
  400.9 8.3 multiply_convert_fusion.16
  426.5 6.8 fusion.89
  457.7 8.2 fusion.80
  486.5 17.6 %all-reduce.1 = bf16[256,512]{1,0:T(8,128)(2,1)} all-reduce(f32[256,512]{1,0:T(8,128)} %fusion.127), channel_id=1, replica_groups=mesh['parts'=2,'tensor'=4,'dp'=4] {'tensor'}, use_global_device_ids=true, to_apply=%region_0.1 | all-reduce | flops 131072 | bytes 786432 | tf_op jit(solution)/shard_map/psum | solution.py:100
  519.4 18.2 %collective-permute-done.27 = bf16[256,2048]{0,1:T(8,128)(2,1)S(1)} collective-permute-done((bf16[256,2048]{0,1:T(8,128)(2,1)}, bf16[256,2048]{0,1:T(8,128)(2,1)S(1)}, u32[]{:S(2)}, u32[]{:S(2)}) %collective-permute-start.27) | collective-permute-done | bytes 1048608 | tf_op jit(solution)/shard_map/ppermute | solution.py:58
  539.7 19.1 %collective-permute-done.33 = bf16[256,2048]{0,1:T(8,128)(2,1)S(1)} collective-permute-done((bf16[256,2048]{0,1:T(8,128)(2,1)S(1)}, bf16[256,2048]{0,1:T(8,128)(2,1)S(1)}, u32[]{:S(2)}, u32[]{:S(2)}) %collective-permute-start.33) | collective-permute-done | bytes 1048608 | tf_op jit(solution)/shard_map/ppermute | solution.py:58
  574.7 91.4 %collective-permute-done.20 = bf16[2048,512]{1,0:T(8,128)(2,1)S(1)} collective-permute-done((bf16[2048,512]{1,0:T(8,128)(2,1)S(1)}, bf16[2048,512]{1,0:T(8,128)(2,1)S(1)}, u32[]{:S(2)}, u32[]{:S(2)}) %collective-permute-start.20) | collective-permute-done | bytes 2097184 | tf_op jit(solution)/shard_map/ppermute | solution.py:72
  669.3 41.7 %collective-permute-done.23 = bf16[2048,512]{1,0:T(8,128)(2,1)S(1)} collective-permute-done((bf16[2048,512]{1,0:T(8,128)(2,1)S(1)}, bf16[2048,512]{1,0:T(8,128)(2,1)S(1)}, u32[]{:S(2)}, u32[]{:S(2)}) %collective-permute-start.23) | collective-permute-done | bytes 2097184 | tf_op jit(solution)/shard_map/ppermute | solution.py:72
  713.0 43.0 %collective-permute-done.26 = bf16[2048,512]{1,0:T(8,128)(2,1)S(1)} collective-permute-done((bf16[2048,512]{1,0:T(8,128)(2,1)S(1)}, bf16[2048,512]{1,0:T(8,128)(2,1)S(1)}, u32[]{:S(2)}, u32[]{:S(2)}) %collective-permute-start.26) | collective-permute-done | bytes 2097184 | tf_op jit(solution)/shard_map/ppermute | solution.py:72
  757.9 44.9 %collective-permute-done.29 = bf16[2048,512]{1,0:T(8,128)(2,1)S(1)} collective-permute-done((bf16[2048,512]{1,0:T(8,128)(2,1)S(1)}, bf16[2048,512]{1,0:T(8,128)(2,1)S(1)}, u32[]{:S(2)}, u32[]{:S(2)}) %collective-permute-start.29) | collective-permute-done | bytes 2097184 | tf_op jit(solution)/shard_map/ppermute | solution.py:72
  806.6 39.3 %collective-permute-done.35 = bf16[2048,512]{1,0:T(8,128)(2,1)S(1)} collective-permute-done((bf16[2048,512]{1,0:T(8,128)(2,1)S(1)}, bf16[2048,512]{1,0:T(8,128)(2,1)S(1)}, u32[]{:S(2)}, u32[]{:S(2)}) %collective-permute-start.35) | collective-permute-done | bytes 2097184 | tf_op jit(solution)/shard_map/ppermute | solution.py:72
  (233 shorter events, 265.8 us)
Async XLA Ops:
  6.9 106.0 %collective-permute-start.10 = (bf16[256,2048]{1,0:T(8,128)(2,1)}, bf16[256,2048]{1,0:T(8,128)(2,1)}, u32[]{:S(2)}, u32[]{:S(2)}) collective-permute-start(bf16[256,2048]{1,0:T(8,128)(2,1)} %get-tuple-element.12), channel_id=1, source_target_pairs={{0,8},{4,12},{8,0},{12,4},{1,9},{5,13},{9,1},{13,5},{2,10},{6,14},... | collective-permute-start | bytes 3145736 | tf_op jit(solution)/shard_map/ppermute | solution.py:29
  9.8 230.9 %collective-permute-start.4 = (bf16[256,2048]{1,0:T(8,128)(2,1)}, bf16[256,2048]{1,0:T(8,128)(2,1)}, u32[]{:S(2)}, u32[]{:S(2)}) collective-permute-start(bf16[256,2048]{1,0:T(8,128)(2,1)} %get-tuple-element.15), channel_id=1, source_target_pairs={{0,8},{4,12},{8,0},{12,4},{1,9},{5,13},{9,1},{13,5},{2,10},{6,14},... | collective-permute-start | bytes 3145736 | tf_op jit(solution)/shard_map/ppermute | solution.py:29
  10.9 56.8 %collective-permute-start = (bf16[256,1024]{1,0:T(8,128)(2,1)S(1)}, bf16[256,1024]{1,0:T(8,128)(2,1)S(1)}, u32[]{:S(2)}, u32[]{:S(2)}) collective-permute-start(bf16[256,1024]{1,0:T(8,128)(2,1)S(1)} %slice.49), channel_id=1, source_target_pairs={{0,8},{4,12},{8,0},{12,4},{1,9},{5,13},{9,1},{13,5},{2,10},{6,14},... | collective-permute-start | bytes 1572872 | tf_op jit(solution)/shard_map/ppermute | solution.py:29
  13.0 59.3 %collective-permute-start.15 = (bf16[256,512]{1,0:T(8,128)(2,1)}, bf16[256,512]{1,0:T(8,128)(2,1)}, u32[]{:S(2)}, u32[]{:S(2)}) collective-permute-start(bf16[256,512]{1,0:T(8,128)(2,1)} %param.5), channel_id=1, source_target_pairs={{0,1},{3,2},{4,5},{7,6},{8,9},{11,10},{12,13},{15,14},{16,17},{19,... | collective-permute-start | bytes 786440 | tf_op jit(solution)/shard_map/ppermute | solution.py:84
  19.4 59.7 %collective-permute-start.36 = (bf16[256,1024]{1,0:T(8,128)(2,1)}, bf16[256,1024]{1,0:T(8,128)(2,1)}, u32[]{:S(2)}, u32[]{:S(2)}) collective-permute-start(bf16[256,1024]{1,0:T(8,128)(2,1)} %convolution_convert_fusion.13), channel_id=1, source_target_pairs={{0,8},{4,12},{8,0},{12,4},{1,9},{5,13},{9,1},{13,5},{2,10},{6,14},... | collective-permute-start | bytes 1572872 | tf_op jit(solution)/shard_map/ppermute | solution.py:29
  72.3 193.1 %collective-permute-start.6 = (bf16[256,2048]{1,0:T(8,128)(2,1)}, bf16[256,2048]{1,0:T(8,128)(2,1)}, u32[]{:S(2)}, u32[]{:S(2)}) collective-permute-start(bf16[256,2048]{1,0:T(8,128)(2,1)} %get-tuple-element.14), channel_id=1, source_target_pairs={{0,8},{4,12},{8,0},{12,4},{1,9},{5,13},{9,1},{13,5},{2,10},{6,14},... | collective-permute-start | bytes 3145736 | tf_op jit(solution)/shard_map/ppermute | solution.py:29
  79.0 186.9 %collective-permute-start.8 = (bf16[256,2048]{1,0:T(8,128)(2,1)}, bf16[256,2048]{1,0:T(8,128)(2,1)}, u32[]{:S(2)}, u32[]{:S(2)}) collective-permute-start(bf16[256,2048]{1,0:T(8,128)(2,1)} %get-tuple-element.13), channel_id=1, source_target_pairs={{0,8},{4,12},{8,0},{12,4},{1,9},{5,13},{9,1},{13,5},{2,10},{6,14},... | collective-permute-start | bytes 3145736 | tf_op jit(solution)/shard_map/ppermute | solution.py:29
  90.1 56.3 %collective-permute-start.38 = (bf16[256,2048]{1,0:T(8,128)(2,1)}, bf16[256,2048]{1,0:T(8,128)(2,1)}, u32[]{:S(2)}, u32[]{:S(2)}) collective-permute-start(bf16[256,2048]{1,0:T(8,128)(2,1)} %convolution_convert_fusion.11), channel_id=1, source_target_pairs={{0,8},{4,12},{8,0},{12,4},{1,9},{5,13},{9,1},{13,5},{2,10},{6,14},... | collective-permute-start | bytes 3145736 | tf_op jit(solution)/shard_map/ppermute | solution.py:29
  112.9 55.9 %collective-permute-start.40 = (bf16[256,2048]{1,0:T(8,128)(2,1)}, bf16[256,2048]{1,0:T(8,128)(2,1)S(1)}, u32[]{:S(2)}, u32[]{:S(2)}) collective-permute-start(bf16[256,2048]{1,0:T(8,128)(2,1)} %convolution_convert_fusion.10), channel_id=1, source_target_pairs={{0,8},{4,12},{8,0},{12,4},{1,9},{5,13},{9,1},{13,5},{2,10},{6,14},... | collective-permute-start | bytes 3145736 | tf_op jit(solution)/shard_map/ppermute | solution.py:29
  266.0 58.0 %collective-permute-start.41 = (bf16[256,2048]{1,0:T(8,128)(2,1)S(1)}, bf16[256,2048]{1,0:T(8,128)(2,1)S(1)}, u32[]{:S(2)}, u32[]{:S(2)}) collective-permute-start(bf16[256,2048]{1,0:T(8,128)(2,1)S(1)} %fusion.51), channel_id=1, source_target_pairs={{0,4},{4,0},{8,12},{12,8},{1,5},{5,1},{9,13},{13,9},{2,6},{6,2},{1... | collective-permute-start | bytes 3145736 | tf_op jit(solution)/shard_map/ppermute | solution.py:29
  324.0 53.8 %collective-permute-start.16 = (bf16[1024,512]{1,0:T(8,128)(2,1)}, bf16[1024,512]{1,0:T(8,128)(2,1)}, u32[]{:S(2)}, u32[]{:S(2)}) collective-permute-start(bf16[1024,512]{1,0:T(8,128)(2,1)} %convolution_convert_fusion.12), channel_id=1, source_target_pairs={{1,2},{2,1},{5,6},{6,5},{9,10},{10,9},{13,14},{14,13},{17,18},{18,... | collective-permute-start | bytes 3145736 | tf_op jit(solution)/shard_map/ppermute | solution.py:69
  333.3 60.0 %collective-permute-start.7 = (bf16[256,2048]{1,0:T(8,128)(2,1)}, bf16[256,2048]{1,0:T(8,128)(2,1)}, u32[]{:S(2)}, u32[]{:S(2)}) collective-permute-start(bf16[256,2048]{1,0:T(8,128)(2,1)} %get-tuple-element.8), channel_id=1, source_target_pairs={{0,4},{4,0},{8,12},{12,8},{1,5},{5,1},{9,13},{13,9},{2,6},{6,2},{1... | collective-permute-start | bytes 3145736 | tf_op jit(solution)/shard_map/ppermute | solution.py:29
  340.9 58.7 %collective-permute-start.5 = (bf16[256,2048]{1,0:T(8,128)(2,1)}, bf16[256,2048]{1,0:T(8,128)(2,1)}, u32[]{:S(2)}, u32[]{:S(2)}) collective-permute-start(bf16[256,2048]{1,0:T(8,128)(2,1)} %get-tuple-element.7), channel_id=1, source_target_pairs={{0,4},{4,0},{8,12},{12,8},{1,5},{5,1},{9,13},{13,9},{2,6},{6,2},{1... | collective-permute-start | bytes 3145736 | tf_op jit(solution)/shard_map/ppermute | solution.py:29
  393.3 87.4 %collective-permute-start.30 = (bf16[256,2048]{0,1:T(8,128)(2,1)S(1)}, bf16[256,2048]{0,1:T(8,128)(2,1)}, u32[]{:S(2)}, u32[]{:S(2)}) collective-permute-start(bf16[256,2048]{0,1:T(8,128)(2,1)S(1)} %bitcast.138), channel_id=1, source_target_pairs={{0,1},{3,2},{4,5},{7,6},{8,9},{11,10},{12,13},{15,14},{16,17},{19,... | collective-permute-start | bytes 3145736 | tf_op jit(solution)/shard_map/ppermute | solution.py:58
  399.6 108.9 %collective-permute-start.17 = (bf16[1024,512]{1,0:T(8,128)(2,1)S(1)}, bf16[1024,512]{1,0:T(8,128)(2,1)}, u32[]{:S(2)}, u32[]{:S(2)}) collective-permute-start(bf16[1024,512]{1,0:T(8,128)(2,1)S(1)} %multiply_convert_fusion.12), channel_id=1, source_target_pairs={{1,0},{2,3},{5,4},{6,7},{9,8},{10,11},{13,12},{14,15},{17,16},{18,... | collective-permute-start | bytes 3145736 | tf_op jit(solution)/shard_map/ppermute | solution.py:72
  419.9 90.0 %collective-permute-start.21 = (bf16[256,2048]{0,1:T(8,128)(2,1)}, bf16[256,2048]{0,1:T(8,128)(2,1)}, u32[]{:S(2)}, u32[]{:S(2)}) collective-permute-start(bf16[256,2048]{0,1:T(8,128)(2,1)} %bitcast.2), channel_id=1, source_target_pairs={{0,1},{3,2},{4,5},{7,6},{8,9},{11,10},{12,13},{15,14},{16,17},{19,... | collective-permute-start | bytes 3145736 | tf_op jit(solution)/shard_map/ppermute | solution.py:58
  484.5 76.6 %collective-permute-start.31 = (bf16[2048,512]{1,0:T(8,128)(2,1)}, bf16[2048,512]{1,0:T(8,128)(2,1)}, u32[]{:S(2)}, u32[]{:S(2)}) collective-permute-start(bf16[2048,512]{1,0:T(8,128)(2,1)} %convolution_convert_fusion.1), channel_id=1, source_target_pairs={{1,2},{2,1},{5,6},{6,5},{9,10},{10,9},{13,14},{14,13},{17,18},{18,... | collective-permute-start | bytes 6291464 | tf_op jit(solution)/shard_map/ppermute | solution.py:69
  509.9 54.9 %collective-permute-start.19 = (bf16[2048,512]{1,0:T(8,128)(2,1)S(1)}, bf16[2048,512]{1,0:T(8,128)(2,1)S(1)}, u32[]{:S(2)}, u32[]{:S(2)}) collective-permute-start(bf16[2048,512]{1,0:T(8,128)(2,1)S(1)} %convolution_convert_fusion.5), channel_id=1, source_target_pairs={{1,2},{2,1},{5,6},{6,5},{9,10},{10,9},{13,14},{14,13},{17,18},{18,... | collective-permute-start | bytes 6291464 | tf_op jit(solution)/shard_map/ppermute | solution.py:69
  564.8 239.9 %collective-permute-start.32 = (bf16[2048,512]{1,0:T(8,128)(2,1)S(1)}, bf16[2048,512]{1,0:T(8,128)(2,1)S(1)}, u32[]{:S(2)}, u32[]{:S(2)}) collective-permute-start(bf16[2048,512]{1,0:T(8,128)(2,1)S(1)} %multiply_convert_fusion.1), channel_id=1, source_target_pairs={{1,0},{2,3},{5,4},{6,7},{9,8},{10,11},{13,12},{14,15},{17,16},{18,... | collective-permute-start | bytes 6291464 | tf_op jit(solution)/shard_map/ppermute | solution.py:72
  566.8 99.3 %collective-permute-start.20 = (bf16[2048,512]{1,0:T(8,128)(2,1)S(1)}, bf16[2048,512]{1,0:T(8,128)(2,1)S(1)}, u32[]{:S(2)}, u32[]{:S(2)}) collective-permute-start(bf16[2048,512]{1,0:T(8,128)(2,1)S(1)} %multiply_convert_fusion.5), channel_id=1, source_target_pairs={{1,0},{2,3},{5,4},{6,7},{9,8},{10,11},{13,12},{14,15},{17,16},{18,... | collective-permute-start | bytes 6291464 | tf_op jit(solution)/shard_map/ppermute | solution.py:72
  568.8 142.3 %collective-permute-start.23 = (bf16[2048,512]{1,0:T(8,128)(2,1)S(1)}, bf16[2048,512]{1,0:T(8,128)(2,1)S(1)}, u32[]{:S(2)}, u32[]{:S(2)}) collective-permute-start(bf16[2048,512]{1,0:T(8,128)(2,1)S(1)} %multiply_convert_fusion.4), channel_id=1, source_target_pairs={{1,0},{2,3},{5,4},{6,7},{9,8},{10,11},{13,12},{14,15},{17,16},{18,... | collective-permute-start | bytes 6291464 | tf_op jit(solution)/shard_map/ppermute | solution.py:72
  570.7 185.3 %collective-permute-start.26 = (bf16[2048,512]{1,0:T(8,128)(2,1)S(1)}, bf16[2048,512]{1,0:T(8,128)(2,1)S(1)}, u32[]{:S(2)}, u32[]{:S(2)}) collective-permute-start(bf16[2048,512]{1,0:T(8,128)(2,1)S(1)} %multiply_convert_fusion.3), channel_id=1, source_target_pairs={{1,0},{2,3},{5,4},{6,7},{9,8},{10,11},{13,12},{14,15},{17,16},{18,... | collective-permute-start | bytes 6291464 | tf_op jit(solution)/shard_map/ppermute | solution.py:72
  572.7 230.1 %collective-permute-start.29 = (bf16[2048,512]{1,0:T(8,128)(2,1)S(1)}, bf16[2048,512]{1,0:T(8,128)(2,1)S(1)}, u32[]{:S(2)}, u32[]{:S(2)}) collective-permute-start(bf16[2048,512]{1,0:T(8,128)(2,1)S(1)} %multiply_convert_fusion.2), channel_id=1, source_target_pairs={{1,0},{2,3},{5,4},{6,7},{9,8},{10,11},{13,12},{14,15},{17,16},{18,... | collective-permute-start | bytes 6291464 | tf_op jit(solution)/shard_map/ppermute | solution.py:72
  666.1 179.8 %collective-permute-start.35 = (bf16[2048,512]{1,0:T(8,128)(2,1)S(1)}, bf16[2048,512]{1,0:T(8,128)(2,1)S(1)}, u32[]{:S(2)}, u32[]{:S(2)}) collective-permute-start(bf16[2048,512]{1,0:T(8,128)(2,1)S(1)} %multiply_convert_fusion), channel_id=1, source_target_pairs={{1,0},{2,3},{5,4},{6,7},{9,8},{10,11},{13,12},{14,15},{17,16},{18,... | collective-permute-start | bytes 6291464 | tf_op jit(solution)/shard_map/ppermute | solution.py:72
  (58 other events, 1727.8 us)

commit v2 on v0

v2 whole, which is shorter than its diff:
```python
import math

import jax
import jax.numpy as jnp
from jax import lax
from jax.experimental import pallas as pl
from jax.experimental.pallas import tpu as pltpu
from jax.sharding import PartitionSpec as P

HAD = 4096
GROUPS = 13
CHUNKS = (1, 1, 2, 2, 2, 2, 2, 1)
BF = jnp.bfloat16
F32 = jnp.float32
ANY = pl.BlockSpec(memory_space=pl.ANY)
SCALARS = pl.BlockSpec(memory_space=pltpu.SMEM)
VMEM_BYTES = 48 * 2**20


def sign_table(order_size, kind):
    indices = jnp.arange(order_size, dtype=jnp.int32)
    intersection = jnp.bitwise_and(indices[:, None], indices[None, :])
    parity_count = jnp.zeros((order_size, order_size), jnp.int32)
    for bit_pos in range(order_size.bit_length() - 1):
        parity_count = parity_count + jnp.bitwise_and(jnp.right_shift(intersection, bit_pos), 1)
    return (1 - 2 * jnp.bitwise_and(parity_count, 1)).astype(kind)


def combined(signs, values, partners):
    current = values.astype(F32)
    for stage, partner in enumerate(partners):
        current = partner.astype(F32) + signs[stage] * current
    return current


def turned(mixed, table):
    base = table.shape[0]
    count = mixed.shape[1] // base
    parts = [
        jnp.dot(mixed[:, i * base:(i + 1) * base], table, preferred_element_type=F32)
        for i in range(count)
    ]
    stride = 1
    while stride < count:
        parts = [
            parts[i] + parts[i ^ stride] if not i & stride else parts[i ^ stride] - parts[i]
            for i in range(count)
        ]
        stride *= 2
    return parts


class Chain:
    def __init__(self):
        self.token = None

    def __call__(self, body, groups, ins, outs, flops=0, aliases=None):
        arrays = [a for a, _ in ins]
        specs = [s for _, s in ins]
        count = len(arrays)
        if self.token is not None:
            arrays.append(self.token)
            specs.append(ANY)
        total = len(arrays)

        def kernel(*refs):
            body(*refs[:count], *refs[total:])

        size = sum(math.prod(s.shape) * s.dtype.itemsize for s, _ in outs)
        results = pl.pallas_call(
            kernel,
            grid=(groups,),
            in_specs=specs,
            out_specs=[s for _, s in outs],
            out_shape=[s for s, _ in outs],
            input_output_aliases=aliases or {},
            compiler_params=pltpu.CompilerParams(vmem_limit_bytes=VMEM_BYTES),
            cost_estimate=pl.CostEstimate(flops=flops, bytes_accessed=3 * size, transcendentals=0),
        )(*arrays)
        self.token = results[0]
        return results


def local(hidden, down_weight, cotangent):
    tensor_size, dp_size = lax.axis_size("tensor"), lax.axis_size("dp")
    position, place = lax.axis_index("tensor"), lax.axis_index("dp")
    last, half = dp_size - 1, dp_size // 2
    rows, width = hidden.shape
    features = cotangent.shape[1]
    unit = width // GROUPS
    table = sign_table(min(unit, 256), BF)
    scale = 1.0 / (rows * dp_size)
    root = 1.0 / math.sqrt(HAD)
    strides = [1 << b for b in reversed(range(tensor_size.bit_length() - 1))]
    stages = len(strides)
    signs = jnp.stack(
        [jnp.where(jnp.bitwise_and(position, s) != 0, -1.0, 1.0).astype(F32) for s in strides]
    )
    chain = Chain()
    starts = [sum(CHUNKS[:j]) for j in range(len(CHUNKS))]
    row_block = (rows, unit)
    grad_block = (unit, features)

    def column(first=0):
        return pl.BlockSpec(row_block, lambda g: (0, first + g))

    def grad_rows(first=0):
        return pl.BlockSpec(grad_block, lambda g: (first + g, 0))

    def whole(array):
        return pl.BlockSpec(array.shape, lambda g: (0,) * array.ndim)

    def strip(j):
        return jax.ShapeDtypeStruct((rows, CHUNKS[j] * unit), BF)

    def grad_shape(j):
        return jax.ShapeDtypeStruct((CHUNKS[j] * unit, features), BF)

    def swap(array, stage):
        stride = strides[stage]
        return lax.ppermute(array, "tensor", [(i, i ^ stride) for i in range(tensor_size)])

    def copied(values, first, j):
        def body(v_ref, o_ref):
            o_ref[...] = v_ref[...]
        return chain(body, CHUNKS[j], [(values, column(first))], [(strip(j), column())])[0]

    def mixed(values, first, partners, j):
        def body(s_ref, v_ref, *refs):
            refs[-1][...] = combined(s_ref, v_ref[...], [r[...] for r in refs[:-1]]).astype(BF)
        ins = [(signs, SCALARS), (values, column(first))] + [(p, column()) for p in partners]
        return chain(body, CHUNKS[j], ins, [(strip(j), column())])[0]

    def rotated_strip(values, first, partners, j, into=None):
        def body(s_ref, v_ref, t_ref, *refs):
            o_ref = refs[-1]
            mix = combined(s_ref, v_ref[...], [r[...] for r in refs[:stages]]) * root
            base = t_ref.shape[0]
            for i, part in enumerate(turned(mix.astype(BF), t_ref[...])):
                o_ref[:, i * base:(i + 1) * base] = part.astype(BF)
        ins = [(signs, SCALARS), (values, column(first)), (table, whole(table))]
        ins += [(p, column()) for p in partners]
        out, spec, aliases = strip(j), column(), None
        if into is not None:
            out, spec = jax.ShapeDtypeStruct((rows, width), BF), column(starts[j])
            if into[0] is not None:
                aliases = {len(ins): 0}
                ins.append((into[0], ANY))
        return chain(
            body, CHUNKS[j], ins, [(out, spec)],
            2 * rows * CHUNKS[j] * unit * table.shape[0], aliases,
        )[0]

    def partial_grad(own, outer, outer_cotangent, j):
        pairs = [(own, cotangent)] + ([(outer, outer_cotangent)] if outer is not None else [])
        def body(*refs):
            total = None
            for k in range(len(pairs)):
                term = lax.dot_general(
                    refs[2 * k][...], refs[2 * k + 1][...], (((0,), (0,)), ((), ())),
                    preferred_element_type=F32,
                )
                total = term if total is None else total + term
            refs[-1][...] = total.astype(BF)
        ins = []
        for r, c in pairs:
            ins += [(r, column()), (c, whole(c))]
        return chain(
            body, CHUNKS[j], ins, [(grad_shape(j), grad_rows())],
            2 * len(pairs) * rows * CHUNKS[j] * unit * features,
        )[0]

    def added(mine, other, factor, j):
        def body(a_ref, b_ref, o_ref):
            o_ref[...] = ((a_ref[...].astype(F32) + b_ref[...].astype(F32)) * factor).astype(BF)
        return chain(
            body, CHUNKS[j], [(mine, grad_rows()), (other, grad_rows())],
            [(grad_shape(j), grad_rows())],
        )[0]

    def placed(total, inners, flags, buffer, j):
        def body(f_ref, t_ref, *refs):
            value = t_ref[...]
            for k in range(len(inners)):
                value = jnp.where(f_ref[k] != 0, refs[k][...], value)
            refs[-1][...] = value
        ins = [(flags, SCALARS), (total, grad_rows())] + [(i, grad_rows()) for i in inners]
        aliases = None
        if buffer is not None:
            aliases = {len(ins): 0}
            ins.append((buffer, ANY))
        return chain(
            body, CHUNKS[j], ins,
            [(jax.ShapeDtypeStruct((width, features), BF), grad_rows(starts[j]))],
            0, aliases,
        )[0]

    def products(rotated, part_out, j):
        def body(c_ref, w_ref, r_ref, *refs):
            back_ref, out_ref = refs[-2:]
            back_ref[...] = lax.dot_general(
                c_ref[...], w_ref[...], (((1,), (1,)), ((), ())), preferred_element_type=F32
            ).astype(BF)

            @pl.when(pl.program_id(0) == 0)
            def _():
                out_ref[...] = refs[0][...] if part_out is not None else jnp.zeros_like(out_ref)

            out_ref[...] += jnp.dot(r_ref[...], w_ref[...], preferred_element_type=F32)
        ins = [(cotangent, whole(cotangent)), (down_weight, grad_rows(starts[j])), (rotated, column())]
        if part_out is not None:
            ins.append((part_out, whole(part_out)))
        shape = jax.ShapeDtypeStruct((rows, features), F32)
        return chain(
            body, CHUNKS[j], ins,
            [(strip(j), column()), (shape, pl.BlockSpec(shape.shape, lambda g: (0, 0)))],
            4 * rows * CHUNKS[j] * unit * features,
        )

    outer_cotangent = None
    if half > 1:
        outer_cotangent = lax.ppermute(cotangent, "dp", [(0, 1), (last, last - 1)])
    flags = jnp.stack([
        ((place == s - 1) | (place == last - s + 1)).astype(jnp.int32) for s in range(half - 1, 0, -1)
    ] or [jnp.int32(0)])

    n = len(CHUNKS)
    got = [[] for _ in range(n)]
    back_got = [[] for _ in range(n)]
    rotated, backs, outer, mine, other, total, inner = ([None] * n for _ in range(7))
    state = {"grad": None, "hidden_grad": None, "out": None}

    def send_hidden(j):
        got[j].append(swap(copied(hidden, starts[j], j), 0))

    def mix_hidden(j, stage):
        got[j].append(swap(mixed(hidden, starts[j], got[j], j), stage))

    def turn_hidden(j):
        rotated[j] = rotated_strip(hidden, starts[j], got[j], j)
        if half > 1:
            outer[j] = lax.ppermute(rotated[j], "dp", [(0, 1), (last, last - 1)])

    def send_partial(j):
        mine[j] = partial_grad(rotated[j], outer[j], outer_cotangent, j)
        for step in range(1, half - 1):
            came = lax.ppermute(mine[j], "dp", [(step, step + 1), (last - step, last - step - 1)])
            mine[j] = added(mine[j], came, 1.0, j)
        other[j] = lax.ppermute(mine[j], "dp", [(half - 1, half), (half, half - 1)])

    def send_total(j):
        total[j] = added(mine[j], other[j], scale, j)
        inner[j] = []
        moving = total[j]
        for step in range(half - 1, 0, -1):
            moving = lax.ppermute(moving, "dp", [(step, step - 1), (last - step, last - step + 1)])
            inner[j].append(moving)

    def place_grad(j):
        state["grad"] = placed(total[j], inner[j], flags, state["grad"], j)

    def send_back(j):
        backs[j], state["out"] = products(rotated[j], state["out"], j)
        back_got[j].append(swap(backs[j], 0))

    def mix_back(j, stage):
        back_got[j].append(swap(mixed(backs[j], 0, back_got[j], j), stage))

    def turn_back(j):
        state["hidden_grad"] = rotated_strip(backs[j], 0, back_got[j], j, (state["hidden_grad"],))

    def on(step, j, *args):
        if 0 <= j < n:
            step(j, *args)

    send_hidden(0)
    on(send_hidden, 1)
    for s in range(1, stages):
        mix_hidden(0, s)
    on(send_hidden, 2)
    turn_hidden(0)
    for s in range(1, stages):
        on(mix_hidden, 1, s)
    on(turn_hidden, 1)
    send_back(0)
    send_partial(0)
    for i in range(n + 1):
        on(send_hidden, i + 3)
        for s in range(1, stages):
            on(mix_hidden, i + 2, s)
            on(mix_back, i, s)
        on(send_back, i + 1)
        on(turn_hidden, i + 2)
        on(send_partial, i + 1)
        on(turn_back, i)
        on(send_total, i)
        on(place_grad, i - 1)
    output = state["out"]
    for stage in range(stages):
        output = output + swap(output, stage)
    return (output.astype(BF), state["grad"], state["hidden_grad"])


def solution(mesh):
    return jax.shard_map(
        local,
        mesh=mesh,
        in_specs=(P(("parts", "dp"), "tensor"), P("tensor", None), P(("parts", "dp"), None)),
        out_specs=(
            P(("parts", "dp"), None),
            P(("parts", "tensor"), None),
            P(("parts", "dp"), "tensor"),
        ),
        check_vma=False,
    )
```

time: 1210 us -> 451 us (0.37)
  waiting for transfers between devices: 1010 us -> 190 us
  Pallas kernels: 0 us -> 142 us
  starting transfers between devices: 5.17 us -> 86.3 us
  matrix products: 69.7 us -> 0 us
  other arithmetic: 44.3 us -> 1.18 us
  blocking collectives: 17.1 us -> 0 us
  local copies, waits for them, and re-layouts: 43 us -> 27.4 us
  between operations: 14.1 us -> 1.63 us
    ppermute x4 -> x59, waiting for transfers between devices: 607 us -> 190 us  [the longest x34 91 us: swap(): lax.ppermute(array, 'tensor', [(i, i ^ stride) for i in range(tensor_size)])]
    reduce_scatter x1 -> x0, waiting for transfers between devices: 407 us -> none  [local(): lax.psum_scatter(part_grad, 'dp', scatter_dimension=0, tiled=True)]
    pallas_call x0 -> x72, Pallas kernels: none -> 142 us  [__call__(): pl.pallas_call(kernel, grid=(groups,), in_specs=specs, out_specs=[s for _...]
    ppermute x4 -> x59, starting transfers between devices: 4.91 us -> 86.3 us  [the longest x8 39.3 us: turn_hidden(): outer[j] = lax.ppermute(rotated[j], 'dp', [(0, 1), (last, last - 1)])]
    dot_general x5 -> x0, matrix products: 69.7 us -> none  [the longest x2 34.3 us: rotate(): jnp.einsum('rcq,qs->rcs', blocks, sign_table(local_size, jnp.bfloat16), p...]
    select_n x2 -> x0, other arithmetic: 24.4 us -> none  [rotate(): current = jnp.where(upper_half, partner - current, current + partner)]
    convert_element_type x3 -> x2, other arithmetic: 19.9 us -> 1.02 us  [the longest x1 0.77 us: local(): return (output.astype(BF), state['grad'], state['hidden_grad'])]
    psum x1 -> x0, blocking collectives: 17.1 us -> none  [local(): output = lax.psum(part_out, 'tensor').astype(jnp.bfloat16)]
  transfers between devices with their start and end apart: 6 -> 59, of which waited for: 4 -> 22; matrix products, arithmetic and copies ran while one was open for 7% -> 3% of each run, Pallas kernels for 0% -> 31%
where the time goes in v2:
time: 451 us; the launch traced here: 449 us
  waiting for transfers between devices  190 us (42%)
  Pallas kernels  142 us (31%)
  starting transfers between devices  86.3 us (19%)
  local copies, waits for them, and re-layouts  27.4 us (6%)
    pallas_call x72, Pallas kernels, __call__(): pl.pallas_call(kernel, grid=(groups,), in_specs=specs, out_specs=[s for _...  142 us
    ppermute x34, waiting for transfers between devices, swap(): lax.ppermute(array, 'tensor', [(i, i ^ stride) for i in range(tensor_size)])  91 us
    ppermute x8, waiting for transfers between devices, send_total(): lax.ppermute(moving, 'dp', [(step, step - 1), (last - step, last - step +...  74.8 us
    ppermute x8, starting transfers between devices, turn_hidden(): outer[j] = lax.ppermute(rotated[j], 'dp', [(0, 1), (last, last - 1)])  39.3 us
    unnamed x75, local copies, waits for them, and re-layouts  27.4 us
    ppermute x34, starting transfers between devices, swap(): lax.ppermute(array, 'tensor', [(i, i ^ stride) for i in range(tensor_size)])  24.6 us
    ppermute x1, waiting for transfers between devices, local(): outer_cotangent = lax.ppermute(cotangent, 'dp', [(0, 1), (last, last - 1)])  12.6 us
    ppermute x8, waiting for transfers between devices, turn_hidden(): outer[j] = lax.ppermute(rotated[j], 'dp', [(0, 1), (last, last - 1)])  11.9 us
  transfers between devices with their start and end apart: 59, of which 22 were waited for; matrix products, arithmetic and copies ran while one was open for 3% of the time, Pallas kernels for 31%

profile of v2, /device:TPU:0, one launch (start us, length us, event | category | flops | bytes accessed | tf_op | source)
XLA Modules:
  0.0 448.9 jit_solution(9724540707049538111)
XLA Ops:
  6.7 10.0 %collective-permute-done.refs_2_.refs_3_ = bf16[256,1024]{1,0:T(8,128)(2,1)S(1)} collective-permute-done((bf16[256,1024]{1,0:T(8,128)(2,1)S(1)}, bf16[256,1024]{1,0:T(8,128)(2,1)S(1)}, u32[]{:S(2)}, u32[]{:S(2)}) %collective-permute-start) | collective-permute-done | bytes 524320 | tf_op jit(solution)/shard_map/ppermute | solution.py:121
  23.2 9.8 %collective-permute-done.5.refs_2_.refs_3_ = bf16[256,1024]{1,0:T(8,128)(2,1)S(1)} collective-permute-done((bf16[256,1024]{1,0:T(8,128)(2,1)}, bf16[256,1024]{1,0:T(8,128)(2,1)S(1)}, u32[]{:S(2)}, u32[]{:S(2)}) %collective-permute-start.5) | collective-permute-done | bytes 524320 | tf_op jit(solution)/shard_map/ppermute | solution.py:121
  42.8 12.6 %collective-permute-done.4.refs_3_ = bf16[256,512]{1,0:T(8,128)(2,1)S(1)} collective-permute-done((bf16[256,512]{1,0:T(8,128)(2,1)S(1)}, bf16[256,512]{1,0:T(8,128)(2,1)S(1)}, u32[]{:S(2)}, u32[]{:S(2)}) %collective-permute-start.4) | collective-permute-done | bytes 262176 | tf_op jit(solution)/shard_map/ppermute | solution.py:222
  61.9 7.2 %collective-permute-start.13 = (bf16[256,1024]{1,0:T(8,128)(2,1)S(1)}, bf16[256,1024]{1,0:T(8,128)(2,1)S(1)}, u32[]{:S(2)}, u32[]{:S(2)}) collective-permute-start(bf16[256,1024]{1,0:T(8,128)(2,1)S(1)} %shard_map.64.refs_3_.refs_2_.refs_0_), channel_id=1, source_target_pairs={{0,1},{3,2},{4,5},{7,6},{8,9},{11,10},{12,13},{15,14},{16,17},{19,... | collective-permute-start | bytes 1572872 | tf_op jit(solution)/shard_map/ppermute | solution.py:242
  69.1 4.7 %collective-permute-done.8.refs_2_.refs_3_ = bf16[256,1024]{1,0:T(8,128)(2,1)S(1)} collective-permute-done((bf16[256,1024]{1,0:T(8,128)(2,1)S(1)}, bf16[256,1024]{1,0:T(8,128)(2,1)S(1)}, u32[]{:S(2)}, u32[]{:S(2)}) %collective-permute-start.8) | collective-permute-done | bytes 524320 | tf_op jit(solution)/shard_map/ppermute | solution.py:121
  78.7 4.5 collective-permute-start.9
  90.6 5.7 %collective-permute-done.10.refs_2_.refs_3_ = bf16[256,2048]{1,0:T(8,128)(2,1)S(1)} collective-permute-done((bf16[256,2048]{1,0:T(8,128)(2,1)S(1)}, bf16[256,2048]{1,0:T(8,128)(2,1)S(1)}, u32[]{:S(2)}, u32[]{:S(2)}) %collective-permute-start.10) | collective-permute-done | bytes 1048608 | tf_op jit(solution)/shard_map/ppermute | solution.py:121
  101.2 5.9 %collective-permute-done.15.refs_2_.refs_3_ = bf16[256,1024]{1,0:T(8,128)(2,1)S(1)} collective-permute-done((bf16[256,1024]{1,0:T(8,128)(2,1)S(1)}, bf16[256,1024]{1,0:T(8,128)(2,1)S(1)}, u32[]{:S(2)}, u32[]{:S(2)}) %collective-permute-start.15) | collective-permute-done | bytes 524320 | tf_op jit(solution)/shard_map/ppermute | solution.py:121
  110.1 4.1 shard_map.78
  135.9 5.7 %collective-permute-start.23 = (bf16[256,2048]{1,0:T(8,128)(2,1)S(1)}, bf16[256,2048]{1,0:T(8,128)(2,1)S(1)}, u32[]{:S(2)}, u32[]{:S(2)}) collective-permute-start(bf16[256,2048]{1,0:T(8,128)(2,1)S(1)} %shard_map.79.refs_4_.refs_2_.refs_0_), channel_id=1, source_target_pairs={{0,1},{3,2},{4,5},{7,6},{8,9},{11,10},{12,13},{15,14},{16,17},{19,... | collective-permute-start | bytes 3145736 | tf_op jit(solution)/shard_map/ppermute | solution.py:242
  141.6 13.0 %collective-permute-done.17.refs_2_.refs_3_ = bf16[256,2048]{1,0:T(8,128)(2,1)} collective-permute-done((bf16[256,2048]{1,0:T(8,128)(2,1)}, bf16[256,2048]{1,0:T(8,128)(2,1)}, u32[]{:S(2)}, u32[]{:S(2)}) %collective-permute-start.17) | collective-permute-done | bytes 1048608 | tf_op jit(solution)/shard_map/ppermute | solution.py:121
  178.6 5.6 %collective-permute-done.26.refs_2_ = bf16[1024,512]{1,0:T(8,128)(2,1)} collective-permute-done((bf16[1024,512]{1,0:T(8,128)(2,1)S(1)}, bf16[1024,512]{1,0:T(8,128)(2,1)}, u32[]{:S(2)}, u32[]{:S(2)}) %collective-permute-start.26) | collective-permute-done | bytes 1048608 | tf_op jit(solution)/shard_map/ppermute | solution.py:256
  193.4 12.8 %collective-permute-done.28.refs_2_.refs_3_ = bf16[256,2048]{1,0:T(8,128)(2,1)} collective-permute-done((bf16[256,2048]{1,0:T(8,128)(2,1)S(1)}, bf16[256,2048]{1,0:T(8,128)(2,1)}, u32[]{:S(2)}, u32[]{:S(2)}) %collective-permute-start.28) | collective-permute-done | bytes 1048608 | tf_op jit(solution)/shard_map/ppermute | solution.py:121
  237.3 7.8 %collective-permute-start.39 = (bf16[256,2048]{1,0:T(8,128)(2,1)S(1)}, bf16[256,2048]{1,0:T(8,128)(2,1)S(1)}, u32[]{:S(2)}, u32[]{:S(2)}) collective-permute-start(bf16[256,2048]{1,0:T(8,128)(2,1)S(1)} %shard_map.97.refs_4_.refs_2_.refs_0_), channel_id=1, source_target_pairs={{0,1},{3,2},{4,5},{7,6},{8,9},{11,10},{12,13},{15,14},{16,17},{19,... | collective-permute-start | bytes 3145736 | tf_op jit(solution)/shard_map/ppermute | solution.py:242
  245.1 10.9 %collective-permute-done.36.refs_2_.refs_3_ = bf16[256,2048]{1,0:T(8,128)(2,1)S(1)} collective-permute-done((bf16[256,2048]{1,0:T(8,128)(2,1)S(1)}, bf16[256,2048]{1,0:T(8,128)(2,1)S(1)}, u32[]{:S(2)}, u32[]{:S(2)}) %collective-permute-start.36) | collective-permute-done | bytes 1048608 | tf_op jit(solution)/shard_map/ppermute | solution.py:121
  275.5 5.9 %collective-permute-start.47 = (bf16[256,2048]{1,0:T(8,128)(2,1)S(1)}, bf16[256,2048]{1,0:T(8,128)(2,1)}, u32[]{:S(2)}, u32[]{:S(2)}) collective-permute-start(bf16[256,2048]{1,0:T(8,128)(2,1)S(1)} %shard_map.106.refs_4_.refs_2_.refs_0_), channel_id=1, source_target_pairs={{0,1},{3,2},{4,5},{7,6},{8,9},{11,10},{12,13},{15,14},{16,17},{19,... | collective-permute-start | bytes 3145736 | tf_op jit(solution)/shard_map/ppermute | solution.py:242
  291.7 6.9 %collective-permute-done.33.refs_2_.refs_3_ = bf16[256,1024]{1,0:T(8,128)(2,1)S(1)} collective-permute-done((bf16[256,1024]{1,0:T(8,128)(2,1)S(1)}, bf16[256,1024]{1,0:T(8,128)(2,1)S(1)}, u32[]{:S(2)}, u32[]{:S(2)}) %collective-permute-start.33) | collective-permute-done | bytes 524320 | tf_op jit(solution)/shard_map/ppermute | solution.py:121
  319.1 18.8 %collective-permute-done.44.refs_2_ = bf16[2048,512]{1,0:T(8,128)(2,1)} collective-permute-done((bf16[2048,512]{1,0:T(8,128)(2,1)}, bf16[2048,512]{1,0:T(8,128)(2,1)}, u32[]{:S(2)}, u32[]{:S(2)}) %collective-permute-start.44) | collective-permute-done | bytes 2097184 | tf_op jit(solution)/shard_map/ppermute | solution.py:256
  347.6 8.6 %collective-permute-done.50.refs_2_ = bf16[256,1024]{1,0:T(8,128)(2,1)S(1)} collective-permute-done((bf16[256,1024]{1,0:T(8,128)(2,1)S(1)}, bf16[256,1024]{1,0:T(8,128)(2,1)S(1)}, u32[]{:S(2)}, u32[]{:S(2)}) %collective-permute-start.50) | collective-permute-done | bytes 524320 | tf_op jit(solution)/shard_map/ppermute | solution.py:242
  365.1 17.7 %collective-permute-done.53.refs_2_ = bf16[2048,512]{1,0:T(8,128)(2,1)} collective-permute-done((bf16[2048,512]{1,0:T(8,128)(2,1)}, bf16[2048,512]{1,0:T(8,128)(2,1)}, u32[]{:S(2)}, u32[]{:S(2)}) %collective-permute-start.53) | collective-permute-done | bytes 2097184 | tf_op jit(solution)/shard_map/ppermute | solution.py:256
  392.3 8.9 %collective-permute-done.48 = f32[256,512]{1,0:T(8,128)S(1)} collective-permute-done((f32[256,512]{1,0:T(8,128)S(1)}, f32[256,512]{1,0:T(8,128)S(1)}, u32[]{:S(2)}, u32[]{:S(2)}) %collective-permute-start.48) | collective-permute-done | bytes 524320 | tf_op jit(solution)/shard_map/ppermute | solution.py:121
  404.0 23.6 %collective-permute-done.58.refs_2_ = bf16[2048,512]{1,0:T(8,128)(2,1)S(1)} collective-permute-done((bf16[2048,512]{1,0:T(8,128)(2,1)S(1)}, bf16[2048,512]{1,0:T(8,128)(2,1)S(1)}, u32[]{:S(2)}, u32[]{:S(2)}) %collective-permute-start.58) | collective-permute-done | bytes 2097184 | tf_op jit(solution)/shard_map/ppermute | solution.py:256
  429.2 10.3 %copy.33.refs_3_ = bf16[13312,512]{1,0:T(8,128)(2,1)} copy(bf16[13312,512]{1,0:T(8,128)(2,1)} %shard_map.128.refs_4_) | data formatting | bytes 27262976
  439.5 8.3 %collective-permute-done.57.refs_2_ = bf16[1024,512]{1,0:T(8,128)(2,1)S(1)} collective-permute-done((bf16[1024,512]{1,0:T(8,128)(2,1)S(1)}, bf16[1024,512]{1,0:T(8,128)(2,1)S(1)}, u32[]{:S(2)}, u32[]{:S(2)}) %collective-permute-start.57) | collective-permute-done | bytes 1048608 | tf_op jit(solution)/shard_map/ppermute | solution.py:256
  (245 shorter events, 217.9 us)
Async XLA Ops:
  21.0 36.4 %collective-permute-start.1 = (bf16[256,2048]{1,0:T(8,128)(2,1)S(1)}, bf16[256,2048]{1,0:T(8,128)(2,1)S(1)}, u32[]{:S(2)}, u32[]{:S(2)}) collective-permute-start(bf16[256,2048]{1,0:T(8,128)(2,1)S(1)} %shard_map.61.refs_5_), channel_id=1, source_target_pairs={{0,8},{4,12},{8,0},{12,4},{1,9},{5,13},{9,1},{13,5},{2,10},{6,14},... | collective-permute-start | bytes 3145736 | tf_op jit(solution)/shard_map/ppermute | solution.py:121
  61.3 35.0 %collective-permute-start.10 = (bf16[256,2048]{1,0:T(8,128)(2,1)S(1)}, bf16[256,2048]{1,0:T(8,128)(2,1)S(1)}, u32[]{:S(2)}, u32[]{:S(2)}) collective-permute-start(bf16[256,2048]{1,0:T(8,128)(2,1)S(1)} %shard_map.67.refs_3_), channel_id=1, source_target_pairs={{0,8},{4,12},{8,0},{12,4},{1,9},{5,13},{9,1},{13,5},{2,10},{6,14},... | collective-permute-start | bytes 3145736 | tf_op jit(solution)/shard_map/ppermute | solution.py:121
  78.7 31.4 %collective-permute-start.9 = (bf16[256,2048]{1,0:T(8,128)(2,1)S(1)}, bf16[256,2048]{1,0:T(8,128)(2,1)S(1)}, u32[]{:S(2)}, u32[]{:S(2)}) collective-permute-start(bf16[256,2048]{1,0:T(8,128)(2,1)S(1)} %shard_map.71.refs_4_.refs_2_.refs_0_), channel_id=1, source_target_pairs={{0,1},{3,2},{4,5},{7,6},{8,9},{11,10},{12,13},{15,14},{16,17},{19,... | collective-permute-start | bytes 3145736 | tf_op jit(solution)/shard_map/ppermute | solution.py:242
  116.0 38.6 %collective-permute-start.17 = (bf16[256,2048]{1,0:T(8,128)(2,1)}, bf16[256,2048]{1,0:T(8,128)(2,1)}, u32[]{:S(2)}, u32[]{:S(2)}) collective-permute-start(bf16[256,2048]{1,0:T(8,128)(2,1)} %get-tuple-element.23.refs_5_.refs_1_), channel_id=1, source_target_pairs={{0,8},{4,12},{8,0},{12,4},{1,9},{5,13},{9,1},{13,5},{2,10},{6,14},... | collective-permute-start | bytes 3145736 | tf_op jit(solution)/shard_map/ppermute | solution.py:121
  122.9 52.5 %collective-permute-start.16 = (bf16[2048,512]{1,0:T(8,128)(2,1)S(1)}, bf16[2048,512]{1,0:T(8,128)(2,1)}, u32[]{:S(2)}, u32[]{:S(2)}) collective-permute-start(bf16[2048,512]{1,0:T(8,128)(2,1)S(1)} %shard_map.80.refs_6_.refs_0_), channel_id=1, source_target_pairs={{1,2},{2,1},{5,6},{6,5},{9,10},{10,9},{13,14},{14,13},{17,18},{18,... | collective-permute-start | bytes 6291464 | tf_op jit(solution)/shard_map/ppermute | solution.py:249
  135.9 30.0 %collective-permute-start.23 = (bf16[256,2048]{1,0:T(8,128)(2,1)S(1)}, bf16[256,2048]{1,0:T(8,128)(2,1)S(1)}, u32[]{:S(2)}, u32[]{:S(2)}) collective-permute-start(bf16[256,2048]{1,0:T(8,128)(2,1)S(1)} %shard_map.79.refs_4_.refs_2_.refs_0_), channel_id=1, source_target_pairs={{0,1},{3,2},{4,5},{7,6},{8,9},{11,10},{12,13},{15,14},{16,17},{19,... | collective-permute-start | bytes 3145736 | tf_op jit(solution)/shard_map/ppermute | solution.py:242
  157.7 30.9 %collective-permute-start.29 = (bf16[256,2048]{1,0:T(8,128)(2,1)}, bf16[256,2048]{1,0:T(8,128)(2,1)}, u32[]{:S(2)}, u32[]{:S(2)}) collective-permute-start(bf16[256,2048]{1,0:T(8,128)(2,1)} %shard_map.84.refs_3_), channel_id=1, source_target_pairs={{0,8},{4,12},{8,0},{12,4},{1,9},{5,13},{9,1},{13,5},{2,10},{6,14},... | collective-permute-start | bytes 3145736 | tf_op jit(solution)/shard_map/ppermute | solution.py:121
  167.0 39.2 %collective-permute-start.28 = (bf16[256,2048]{1,0:T(8,128)(2,1)S(1)}, bf16[256,2048]{1,0:T(8,128)(2,1)}, u32[]{:S(2)}, u32[]{:S(2)}) collective-permute-start(bf16[256,2048]{1,0:T(8,128)(2,1)S(1)} %get-tuple-element.25.refs_5_.refs_1_), channel_id=1, source_target_pairs={{0,8},{4,12},{8,0},{12,4},{1,9},{5,13},{9,1},{13,5},{2,10},{6,14},... | collective-permute-start | bytes 3145736 | tf_op jit(solution)/shard_map/ppermute | solution.py:121
  170.4 57.0 %collective-permute-start.27 = (bf16[2048,512]{1,0:T(8,128)(2,1)S(1)}, bf16[2048,512]{1,0:T(8,128)(2,1)}, u32[]{:S(2)}, u32[]{:S(2)}) collective-permute-start(bf16[2048,512]{1,0:T(8,128)(2,1)S(1)} %shard_map.89.refs_6_.refs_0_), channel_id=1, source_target_pairs={{1,2},{2,1},{5,6},{6,5},{9,10},{10,9},{13,14},{14,13},{17,18},{18,... | collective-permute-start | bytes 6291464 | tf_op jit(solution)/shard_map/ppermute | solution.py:249
  177.3 54.3 %collective-permute-start.25 = (bf16[2048,512]{1,0:T(8,128)(2,1)S(1)}, bf16[2048,512]{1,0:T(8,128)(2,1)}, u32[]{:S(2)}, u32[]{:S(2)}) collective-permute-start(bf16[2048,512]{1,0:T(8,128)(2,1)S(1)} %shard_map.91.refs_4_.refs_1_), channel_id=1, source_target_pairs={{1,0},{2,3},{5,4},{6,7},{9,8},{10,11},{13,12},{14,15},{17,16},{18,... | collective-permute-start | bytes 6291464 | tf_op jit(solution)/shard_map/ppermute | solution.py:256
  220.1 53.9 %collective-permute-start.35 = (bf16[2048,512]{1,0:T(8,128)(2,1)S(1)}, bf16[2048,512]{1,0:T(8,128)(2,1)S(1)}, u32[]{:S(2)}, u32[]{:S(2)}) collective-permute-start(bf16[2048,512]{1,0:T(8,128)(2,1)S(1)} %shard_map.98.refs_6_.refs_0_), channel_id=1, source_target_pairs={{1,2},{2,1},{5,6},{6,5},{9,10},{10,9},{13,14},{14,13},{17,18},{18,... | collective-permute-start | bytes 6291464 | tf_op jit(solution)/shard_map/ppermute | solution.py:249
  221.9 34.1 %collective-permute-start.36 = (bf16[256,2048]{1,0:T(8,128)(2,1)S(1)}, bf16[256,2048]{1,0:T(8,128)(2,1)S(1)}, u32[]{:S(2)}, u32[]{:S(2)}) collective-permute-start(bf16[256,2048]{1,0:T(8,128)(2,1)S(1)} %get-tuple-element.27.refs_5_.refs_1_), channel_id=1, source_target_pairs={{0,8},{4,12},{8,0},{12,4},{1,9},{5,13},{9,1},{13,5},{2,10},{6,14},... | collective-permute-start | bytes 3145736 | tf_op jit(solution)/shard_map/ppermute | solution.py:121
  230.3 56.8 %collective-permute-start.34 = (bf16[2048,512]{1,0:T(8,128)(2,1)}, bf16[2048,512]{1,0:T(8,128)(2,1)}, u32[]{:S(2)}, u32[]{:S(2)}) collective-permute-start(bf16[2048,512]{1,0:T(8,128)(2,1)} %shard_map.100.refs_4_.refs_1_), channel_id=1, source_target_pairs={{1,0},{2,3},{5,4},{6,7},{9,8},{10,11},{13,12},{14,15},{17,16},{18,... | collective-permute-start | bytes 6291464 | tf_op jit(solution)/shard_map/ppermute | solution.py:256
  237.3 30.7 %collective-permute-start.39 = (bf16[256,2048]{1,0:T(8,128)(2,1)S(1)}, bf16[256,2048]{1,0:T(8,128)(2,1)S(1)}, u32[]{:S(2)}, u32[]{:S(2)}) collective-permute-start(bf16[256,2048]{1,0:T(8,128)(2,1)S(1)} %shard_map.97.refs_4_.refs_2_.refs_0_), channel_id=1, source_target_pairs={{0,1},{3,2},{4,5},{7,6},{8,9},{11,10},{12,13},{15,14},{16,17},{19,... | collective-permute-start | bytes 3145736 | tf_op jit(solution)/shard_map/ppermute | solution.py:242
  261.8 38.3 %collective-permute-start.42 = (bf16[256,2048]{1,0:T(8,128)(2,1)S(1)}, bf16[256,2048]{1,0:T(8,128)(2,1)}, u32[]{:S(2)}, u32[]{:S(2)}) collective-permute-start(bf16[256,2048]{1,0:T(8,128)(2,1)S(1)} %get-tuple-element.29.refs_5_.refs_1_), channel_id=1, source_target_pairs={{0,8},{4,12},{8,0},{12,4},{1,9},{5,13},{9,1},{13,5},{2,10},{6,14},... | collective-permute-start | bytes 3145736 | tf_op jit(solution)/shard_map/ppermute | solution.py:121
  272.0 42.9 %collective-permute-start.45 = (bf16[2048,512]{1,0:T(8,128)(2,1)S(1)}, bf16[2048,512]{1,0:T(8,128)(2,1)}, u32[]{:S(2)}, u32[]{:S(2)}) collective-permute-start(bf16[2048,512]{1,0:T(8,128)(2,1)S(1)} %shard_map.107.refs_6_.refs_0_), channel_id=1, source_target_pairs={{1,2},{2,1},{5,6},{6,5},{9,10},{10,9},{13,14},{14,13},{17,18},{18,... | collective-permute-start | bytes 6291464 | tf_op jit(solution)/shard_map/ppermute | solution.py:249
  275.5 32.9 %collective-permute-start.47 = (bf16[256,2048]{1,0:T(8,128)(2,1)S(1)}, bf16[256,2048]{1,0:T(8,128)(2,1)}, u32[]{:S(2)}, u32[]{:S(2)}) collective-permute-start(bf16[256,2048]{1,0:T(8,128)(2,1)S(1)} %shard_map.106.refs_4_.refs_2_.refs_0_), channel_id=1, source_target_pairs={{0,1},{3,2},{4,5},{7,6},{8,9},{11,10},{12,13},{15,14},{16,17},{19,... | collective-permute-start | bytes 3145736 | tf_op jit(solution)/shard_map/ppermute | solution.py:242
  287.1 50.8 %collective-permute-start.44 = (bf16[2048,512]{1,0:T(8,128)(2,1)}, bf16[2048,512]{1,0:T(8,128)(2,1)}, u32[]{:S(2)}, u32[]{:S(2)}) collective-permute-start(bf16[2048,512]{1,0:T(8,128)(2,1)} %shard_map.109.refs_4_.refs_1_), channel_id=1, source_target_pairs={{1,0},{2,3},{5,4},{6,7},{9,8},{10,11},{13,12},{14,15},{17,16},{18,... | collective-permute-start | bytes 6291464 | tf_op jit(solution)/shard_map/ppermute | solution.py:256
  305.4 35.8 %collective-permute-start.43 = (bf16[256,2048]{1,0:T(8,128)(2,1)S(1)}, bf16[256,2048]{1,0:T(8,128)(2,1)}, u32[]{:S(2)}, u32[]{:S(2)}) collective-permute-start(bf16[256,2048]{1,0:T(8,128)(2,1)S(1)} %get-tuple-element.31.refs_5_.refs_1_), channel_id=1, source_target_pairs={{0,8},{4,12},{8,0},{12,4},{1,9},{5,13},{9,1},{13,5},{2,10},{6,14},... | collective-permute-start | bytes 3145736 | tf_op jit(solution)/shard_map/ppermute | solution.py:121
  311.1 48.7 %collective-permute-start.54 = (bf16[2048,512]{1,0:T(8,128)(2,1)S(1)}, bf16[2048,512]{1,0:T(8,128)(2,1)S(1)}, u32[]{:S(2)}, u32[]{:S(2)}) collective-permute-start(bf16[2048,512]{1,0:T(8,128)(2,1)S(1)} %shard_map.115.refs_6_.refs_0_), channel_id=1, source_target_pairs={{1,2},{2,1},{5,6},{6,5},{9,10},{10,9},{13,14},{14,13},{17,18},{18,... | collective-permute-start | bytes 6291464 | tf_op jit(solution)/shard_map/ppermute | solution.py:249
  317.8 65.1 %collective-permute-start.53 = (bf16[2048,512]{1,0:T(8,128)(2,1)}, bf16[2048,512]{1,0:T(8,128)(2,1)}, u32[]{:S(2)}, u32[]{:S(2)}) collective-permute-start(bf16[2048,512]{1,0:T(8,128)(2,1)} %shard_map.117.refs_4_.refs_1_), channel_id=1, source_target_pairs={{1,0},{2,3},{5,4},{6,7},{9,8},{10,11},{13,12},{14,15},{17,16},{18,... | collective-permute-start | bytes 6291464 | tf_op jit(solution)/shard_map/ppermute | solution.py:256
  346.3 39.8 %collective-permute-start.52 = (bf16[256,1024]{1,0:T(8,128)(2,1)S(1)}, bf16[256,1024]{1,0:T(8,128)(2,1)S(1)}, u32[]{:S(2)}, u32[]{:S(2)}) collective-permute-start(bf16[256,1024]{1,0:T(8,128)(2,1)S(1)} %get-tuple-element.34.refs_4_.refs_1_), channel_id=1, source_target_pairs={{0,8},{4,12},{8,0},{12,4},{1,9},{5,13},{9,1},{13,5},{2,10},{6,14},... | collective-permute-start | bytes 1572872 | tf_op jit(solution)/shard_map/ppermute | solution.py:121
  363.1 64.6 %collective-permute-start.58 = (bf16[2048,512]{1,0:T(8,128)(2,1)S(1)}, bf16[2048,512]{1,0:T(8,128)(2,1)S(1)}, u32[]{:S(2)}, u32[]{:S(2)}) collective-permute-start(bf16[2048,512]{1,0:T(8,128)(2,1)S(1)} %shard_map.123.refs_4_.refs_1_), channel_id=1, source_target_pairs={{1,0},{2,3},{5,4},{6,7},{9,8},{10,11},{13,12},{14,15},{17,16},{18,... | collective-permute-start | bytes 6291464 | tf_op jit(solution)/shard_map/ppermute | solution.py:256
  390.9 56.9 %collective-permute-start.57 = (bf16[1024,512]{1,0:T(8,128)(2,1)S(1)}, bf16[1024,512]{1,0:T(8,128)(2,1)S(1)}, u32[]{:S(2)}, u32[]{:S(2)}) collective-permute-start(bf16[1024,512]{1,0:T(8,128)(2,1)S(1)} %shard_map.127.refs_4_.refs_1_), channel_id=1, source_target_pairs={{1,0},{2,3},{5,4},{6,7},{9,8},{10,11},{13,12},{14,15},{17,16},{18,... | collective-permute-start | bytes 3145736 | tf_op jit(solution)/shard_map/ppermute | solution.py:256
  (72 other events, 874.2 us)

commit v3 on v2

v3 whole, which is shorter than its diff:
```python
import math

import jax
import jax.numpy as jnp
from jax import lax
from jax.experimental import pallas as pl
from jax.experimental.pallas import tpu as pltpu
from jax.sharding import PartitionSpec as P

HAD = 4096
GROUPS = 13
CHUNKS = (1, 1, 2, 2, 2, 2, 2, 1)
LAG = 3
BF = jnp.bfloat16
F32 = jnp.float32
ANY = pl.BlockSpec(memory_space=pl.ANY)
SCALARS = pl.BlockSpec(memory_space=pltpu.SMEM)
VMEM_BYTES = 48 * 2**20


def sign_table(order_size, kind):
    indices = jnp.arange(order_size, dtype=jnp.int32)
    intersection = jnp.bitwise_and(indices[:, None], indices[None, :])
    parity_count = jnp.zeros((order_size, order_size), jnp.int32)
    for bit_pos in range(order_size.bit_length() - 1):
        parity_count = parity_count + jnp.bitwise_and(jnp.right_shift(intersection, bit_pos), 1)
    return (1 - 2 * jnp.bitwise_and(parity_count, 1)).astype(kind)


def turned(mixed, table):
    base = table.shape[0]
    count = mixed.shape[1] // base
    parts = [
        jnp.dot(mixed[:, i * base:(i + 1) * base], table, preferred_element_type=F32)
        for i in range(count)
    ]
    stride = 1
    while stride < count:
        parts = [
            parts[i] + parts[i ^ stride] if not i & stride else parts[i ^ stride] - parts[i]
            for i in range(count)
        ]
        stride *= 2
    return parts


class Chain:
    def __init__(self):
        self.token = None
        self.after = []

    def __call__(self, name, body, groups, ins, outs, aliases=None):
        arrays = [a for a, _ in ins]
        specs = [s for _, s in ins]
        count = len(arrays)
        for late in [self.token] + self.after:
            if late is not None and all(a is not late for a in arrays):
                arrays.append(late)
                specs.append(ANY)
        self.after = []
        total = len(arrays)

        def kernel(*refs):
            body(*refs[:count], *refs[total:])

        results = pl.pallas_call(
            kernel,
            grid=(groups,),
            name=name,
            in_specs=specs,
            out_specs=[s for _, s in outs],
            out_shape=[s for s, _ in outs],
            input_output_aliases=aliases or {},
            compiler_params=pltpu.CompilerParams(vmem_limit_bytes=VMEM_BYTES),
            cost_estimate=pl.CostEstimate(flops=1, bytes_accessed=1, transcendentals=0),
        )(*arrays)
        self.token = results[0]
        return results


def local(hidden, down_weight, cotangent):
    tensor_size, dp_size = lax.axis_size("tensor"), lax.axis_size("dp")
    position, place = lax.axis_index("tensor"), lax.axis_index("dp")
    last, half = dp_size - 1, dp_size // 2
    rows, width = hidden.shape
    features = cotangent.shape[1]
    unit = width // GROUPS
    table = sign_table(min(unit, 256), BF)
    scale = 1.0 / (rows * dp_size)
    root = 1.0 / math.sqrt(HAD)
    strides = [1 << b for b in reversed(range(tensor_size.bit_length() - 1))]
    stages = len(strides) - 1
    signs = jnp.stack(
        [jnp.where(jnp.bitwise_and(position, s) != 0, -1.0, 1.0).astype(F32) for s in strides]
    )
    chain = Chain()
    starts = [sum(CHUNKS[:j]) for j in range(len(CHUNKS))]
    row_block = (rows, unit)
    grad_block = (unit, features)

    def column(first=0):
        return pl.BlockSpec(row_block, lambda g: (0, first + g))

    def grad_rows(first=0):
        return pl.BlockSpec(grad_block, lambda g: (first + g, 0))

    def whole(array):
        return pl.BlockSpec(array.shape, lambda g: (0,) * array.ndim)

    def grad_shape(j):
        return jax.ShapeDtypeStruct((CHUNKS[j] * unit, features), BF)

    def swap(array, stage):
        stride = strides[stage]
        pairs = [(i, i ^ stride) for i in range(tensor_size)]
        if isinstance(array, (list, tuple)):
            return [lax.ppermute(a, "tensor", pairs) for a in array]
        return lax.ppermute(array, "tensor", pairs)

    def copied(j, size):
        def body(v_ref, o_ref):
            o_ref[...] = v_ref[...]
        shape = jax.ShapeDtypeStruct((rows, size * unit), BF)
        return chain(
            "copied", body, CHUNKS[j], [(hidden, column(starts[j]))], [(shape, column())]
        )[0]

    def across(refs, partners):
        current = refs[1][...].astype(F32)
        for stage in range(partners):
            current = refs[2 + stage][...].astype(F32) + refs[0][stage] * current
        return current

    def mixed(own, count, partners):
        def body(*refs):
            refs[-1][...] = across(refs, len(partners)).astype(BF)
        ins = [(signs, SCALARS)] + [(v, column(at)) for v, at in [own] + partners]
        shape = jax.ShapeDtypeStruct((rows, count * unit), BF)
        return chain("mixed", body, count, ins, [(shape, column())])[0]

    def rotated_strip(own, count, partners, into=None, at=0):
        def body(*refs):
            o_ref, t_ref = refs[-1], refs[table_at]
            base = t_ref.shape[0]
            mix = (across(refs, stages) * root).astype(BF)
            for i, part in enumerate(turned(mix, t_ref[...])):
                o_ref[:, i * base:(i + 1) * base] = part.astype(BF)
        ins = [(signs, SCALARS)] + [(v, column(first)) for v, first in [own] + partners]
        table_at = len(ins)
        ins.append((table, whole(table)))
        out = jax.ShapeDtypeStruct((rows, count * unit if into is None else width), BF)
        aliases = None
        if into is not None and into[0] is not None:
            aliases = {len(ins): 0}
            ins.append((into[0], ANY))
        return chain("rotated", body, count, ins, [(out, column(at))], aliases)[0]

    def partial_grad(own, outer, outer_cotangent, j):
        pairs = [(own, cotangent)] + ([(outer, outer_cotangent)] if outer is not None else [])
        def body(*refs):
            total = None
            for k in range(len(pairs)):
                term = lax.dot_general(
                    refs[2 * k][...], refs[2 * k + 1][...], (((0,), (0,)), ((), ())),
                    preferred_element_type=F32,
                )
                total = term if total is None else total + term
            refs[-1][...] = total.astype(BF)
        ins = []
        for r, c in pairs:
            ins += [(r, column()), (c, whole(c))]
        return chain(
            "partial_grad", body, CHUNKS[j], ins, [(grad_shape(j), grad_rows())],
        )[0]

    def added(mine, other, factor, j):
        def body(a_ref, b_ref, o_ref):
            o_ref[...] = ((a_ref[...].astype(F32) + b_ref[...].astype(F32)) * factor).astype(BF)
        return chain(
            "added", body, CHUNKS[j], [(mine, grad_rows()), (other, grad_rows())],
            [(grad_shape(j), grad_rows())],
        )[0]

    def chosen(total, inners, j):
        def body(f_ref, t_ref, *refs):
            value = t_ref[...]
            for k in range(len(inners)):
                value = jnp.where(f_ref[k] != 0, refs[k][...], value)
            refs[-1][...] = value
        ins = [(flags, SCALARS), (total, grad_rows())] + [(i, grad_rows()) for i in inners]
        return chain("chosen", body, CHUNKS[j], ins, [(grad_shape(j), grad_rows())])[0]

    def placed(mine, partner, buffer, j):
        def body(s_ref, a_ref, b_ref, *refs):
            value = b_ref[...].astype(F32) + s_ref[stages] * a_ref[...].astype(F32)
            refs[-1][...] = value.astype(BF)
        ins = [(signs, SCALARS), (mine, grad_rows()), (partner, grad_rows())]
        aliases = None
        if buffer is not None:
            aliases = {len(ins): 0}
            ins.append((buffer, ANY))
        return chain(
            "placed", body, CHUNKS[j], ins,
            [(jax.ShapeDtypeStruct((width, features), BF), grad_rows(starts[j]))],
            aliases,
        )[0]

    def products(rotated, part_out, buffer, first, size, j):
        def body(s_ref, c_ref, w_ref, p_ref, r_ref, *refs):
            back_ref, out_ref = refs[-2:]
            weights = (
                p_ref[...].astype(F32) + s_ref[stages] * w_ref[...].astype(F32)
            ).astype(BF)
            back_ref[...] = lax.dot_general(
                c_ref[...], weights, (((1,), (1,)), ((), ())), preferred_element_type=F32
            ).astype(BF)

            @pl.when(pl.program_id(0) == 0)
            def _():
                out_ref[...] = refs[0][...] if part_out is not None else jnp.zeros_like(out_ref)

            out_ref[...] += jnp.dot(r_ref[...], weights, preferred_element_type=F32)
        ins = [
            (signs, SCALARS), (cotangent, whole(cotangent)), (down_weight, grad_rows(starts[j])),
            (weight_partner, grad_rows(starts[j])), (rotated, column()),
        ]
        aliases = {}
        if part_out is not None:
            aliases[len(ins)] = 1
            ins.append((part_out, whole(part_out)))
        if buffer is not None:
            aliases[len(ins)] = 0
            ins.append((buffer, ANY))
        shape = jax.ShapeDtypeStruct((rows, features), F32)
        return chain(
            "products", body, CHUNKS[j], ins,
            [(jax.ShapeDtypeStruct((rows, size * unit), BF), column(first)),
             (shape, pl.BlockSpec(shape.shape, lambda g: (0, 0)))],
            aliases,
        )

    def joined(mine, other, kind):
        def body(a_ref, b_ref, o_ref):
            o_ref[...] = (a_ref[...] + b_ref[...]).astype(kind)
        return chain(
            "joined", body, 1, [(mine, whole(mine)), (other, whole(other))],
            [(jax.ShapeDtypeStruct(mine.shape, kind), whole(mine))],
        )[0]

    weight_partner = swap(down_weight, stages)
    outer_cotangent = None
    if half > 1:
        outer_cotangent = lax.ppermute(cotangent, "dp", [(0, 1), (last, last - 1)])
    flags = jnp.stack([
        ((place == s - 1) | (place == last - s + 1)).astype(jnp.int32) for s in range(half - 1, 0, -1)
    ] or [jnp.int32(0)])

    n = len(CHUNKS)
    sent = {}
    rotated, outer, mine, other, total, inner, whole_sum, partner_sum = (
        [None] * n for _ in range(8)
    )
    state = {"grad": None, "hidden_grad": None, "out": None}
    total_out = []

    def send(r):
        b = r - LAG
        ahead = CHUNKS[r] if r < n else 0
        size = ahead + (CHUNKS[b] if b >= 0 else 0)
        buffer = copied(r, size) if r < n else None
        if b >= 0:
            buffer, state["out"] = products(rotated[b], state["out"], buffer, ahead, size, b)
            if b == n - 1:
                total_out.append((state["out"], swap(state["out"], 0)))
        sent[r] = []
        came = swap(buffer, 0) if stages else None
        for own, groups, at in ((hidden, ahead, 0), (buffer, size - ahead, ahead)):
            first = starts[r] if own is hidden and groups else at
            sent[r].append(((own, first), groups, [(came, at)] if stages else []))

    def mix(r):
        for s in range(1, stages):
            for own, groups, came in sent[r]:
                if groups:
                    came.append((swap(mixed(own, groups, came), s), 0))

    def turn(r):
        own, groups, came = sent[r][0]
        rotated[r] = rotated_strip(own, groups, came)
        if half > 1:
            outer[r] = lax.ppermute(rotated[r], "dp", [(0, 1), (last, last - 1)])

    def turn_back(b):
        own, groups, came = sent[b + LAG][1]
        state["hidden_grad"] = rotated_strip(
            own, groups, came, (state["hidden_grad"],), starts[b]
        )

    def send_partial(j):
        mine[j] = partial_grad(rotated[j], outer[j], outer_cotangent, j)
        for step in range(1, half - 1):
            came = lax.ppermute(mine[j], "dp", [(step, step + 1), (last - step, last - step - 1)])
            mine[j] = added(mine[j], came, 1.0, j)
        other[j] = lax.ppermute(mine[j], "dp", [(half - 1, half), (half, half - 1)])

    def send_total(j):
        total[j] = added(mine[j], other[j], scale, j)
        inner[j] = []
        moving = total[j]
        for step in range(half - 1, 0, -1):
            moving = lax.ppermute(moving, "dp", [(step, step - 1), (last - step, last - step + 1)])
            inner[j].append(moving)

    def choose(j):
        whole_sum[j] = chosen(total[j], inner[j], j)
        partner_sum[j] = swap(whole_sum[j], stages)

    def place_grad(j):
        state["grad"] = placed(whole_sum[j], partner_sum[j], state["grad"], j)

    def on(step, j, end=n):
        if 0 <= j < end:
            step(j)

    send(0)
    send(1)
    mix(0)
    chain.after = [outer_cotangent]
    turn(0)
    send(2)
    mix(1)
    turn(1)
    send_partial(0)
    send(3)
    send_partial(1)
    mix(2)
    turn(2)
    send_total(0)
    def join(stage):
        mine, came = total_out[-1]
        output = joined(mine, came, F32 if stage < stages else BF)
        total_out.append((output, swap(output, stage + 1) if stage < stages else None))

    for r in range(3, n + LAG + 1):
        on(send, r + 1, n + LAG)
        on(send_partial, r - 1)
        if r == 3:
            choose(0)
        if r >= n:
            on(mix, r, n + LAG)
            on(turn_back, r - LAG)
        if r == n + LAG - 1:
            for stage in range(stages + 1):
                join(stage)
        on(send_total, r - 2)
        on(mix, r)
        on(turn, r)
        if r > 3:
            on(choose, r - 3)
        on(place_grad, r - 4)
        if r < n:
            turn_back(r - LAG)
    return (total_out[-1][0], state["grad"], state["hidden_grad"])


def solution(mesh):
    return jax.shard_map(
        local,
        mesh=mesh,
        in_specs=(P(("parts", "dp"), "tensor"), P("tensor", None), P(("parts", "dp"), None)),
        out_specs=(
            P(("parts", "dp"), None),
            P(("parts", "tensor"), None),
            P(("parts", "dp"), "tensor"),
        ),
        check_vma=False,
    )
```

time: 451 us -> 407 us (0.902)
  waiting for transfers between devices: 190 us -> 158 us
  local copies, waits for them, and re-layouts: 27.4 us -> 10.5 us
    unnamed x75 -> x52, local copies, waits for them, and re-layouts: 27.4 us -> 10.5 us
    ppermute x8, waiting for transfers between devices: 74.8 us -> 59.8 us  [send_total(): lax.ppermute(moving, 'dp', [(step, step - 1), (last - step, last - step +...]
    ppermute x42 -> x30, waiting for transfers between devices: 103 us -> 94.1 us  [the longest x22 53.8 us: swap(): return lax.ppermute(array, 'tensor', pairs)]
    ppermute x1, waiting for transfers between devices: 12.6 us -> 3.9 us  [local(): outer_cotangent = lax.ppermute(cotangent, 'dp', [(0, 1), (last, last - 1)])]
    pallas_call x72 -> x66, Pallas kernels: 142 us -> 146 us  [__call__(): pl.pallas_call(kernel, grid=(groups,), name=name, in_specs=specs, out_spe...]
    ppermute x42 -> x30, starting transfers between devices: 63.9 us -> 61.2 us  [the longest x8 46.5 us: turn(): outer[r] = lax.ppermute(rotated[r], 'dp', [(0, 1), (last, last - 1)])]
  transfers between devices with their start and end apart: 59 -> 47, of which waited for: 22 -> 22; matrix products, arithmetic and copies ran while one was open for 3% -> 0% of each run, Pallas kernels for 31% -> 36%
where the time goes in v3:
time: 407 us; the launch traced here: 405 us
  waiting for transfers between devices  158 us (39%)
  Pallas kernels  146 us (36%)
  starting transfers between devices  89.5 us (22%)
  local copies, waits for them, and re-layouts  10.5 us (3%)
    pallas_call x66, Pallas kernels, __call__(): pl.pallas_call(kernel, grid=(groups,), name=name, in_specs=specs, out_spe...  146 us
    ppermute x8, waiting for transfers between devices, send_total(): lax.ppermute(moving, 'dp', [(step, step - 1), (last - step, last - step +...  59.8 us
    ppermute x22, waiting for transfers between devices, swap(): return lax.ppermute(array, 'tensor', pairs)  53.8 us
    ppermute x8, starting transfers between devices, turn(): outer[r] = lax.ppermute(rotated[r], 'dp', [(0, 1), (last, last - 1)])  46.5 us
    ppermute x8, waiting for transfers between devices, turn(): outer[r] = lax.ppermute(rotated[r], 'dp', [(0, 1), (last, last - 1)])  40.3 us
    ppermute x22, starting transfers between devices, swap(): return lax.ppermute(array, 'tensor', pairs)  14.7 us
    ppermute x8, starting transfers between devices, send_partial(): other[j] = lax.ppermute(mine[j], 'dp', [(half - 1, half), (half, half - 1)])  14 us
    ppermute x8, starting transfers between devices, send_total(): lax.ppermute(moving, 'dp', [(step, step - 1), (last - step, last - step +...  10.8 us
  transfers between devices with their start and end apart: 47, of which 22 were waited for; matrix products, arithmetic and copies ran while one was open for 0% of the time, Pallas kernels for 36%

profile of v3, /device:TPU:0, one launch (start us, length us, event | category | flops | bytes accessed | tf_op | source)
XLA Modules:
  0.0 405.4 jit_solution(3276211092236760591)
XLA Ops:
  10.3 3.9 collective-permute-done.3.refs_5_.refs_3_
  19.0 4.0 collective-permute-start.4
  35.0 7.2 %collective-permute-start.7 = (bf16[256,1024]{1,0:T(8,128)(2,1)S(1)}, bf16[256,1024]{1,0:T(8,128)(2,1)S(1)}, u32[]{:S(2)}, u32[]{:S(2)}) collective-permute-start(bf16[256,1024]{1,0:T(8,128)(2,1)S(1)} %rotated.17.refs_4_.refs_0_), channel_id=1, source_target_pairs={{0,1},{3,2},{4,5},{7,6},{8,9},{11,10},{12,13},{15,14},{16,17},{19,... | collective-permute-start | bytes 1572872 | tf_op jit(solution)/shard_map/ppermute | solution.py:291
  55.2 4.5 %collective-permute-start.9 = (bf16[256,2048]{1,0:T(8,128)(2,1)S(1)}, bf16[256,2048]{1,0:T(8,128)(2,1)S(1)}, u32[]{:S(2)}, u32[]{:S(2)}) collective-permute-start(bf16[256,2048]{1,0:T(8,128)(2,1)S(1)} %rotated.18.refs_2_.refs_0_.refs_4_), channel_id=1, source_target_pairs={{0,1},{3,2},{4,5},{7,6},{8,9},{11,10},{12,13},{15,14},{16,17},{19,... | collective-permute-start | bytes 3145736 | tf_op jit(solution)/shard_map/ppermute | solution.py:291
  67.6 11.8 %collective-permute-done.9.refs_2_ = bf16[256,2048]{1,0:T(8,128)(2,1)S(1)} collective-permute-done((bf16[256,2048]{1,0:T(8,128)(2,1)S(1)}, bf16[256,2048]{1,0:T(8,128)(2,1)S(1)}, u32[]{:S(2)}, u32[]{:S(2)}) %collective-permute-start.9) | collective-permute-done | bytes 1048608 | tf_op jit(solution)/shard_map/ppermute | solution.py:291
  95.0 6.0 %collective-permute-start.14 = (bf16[256,2048]{1,0:T(8,128)(2,1)S(1)}, bf16[256,2048]{1,0:T(8,128)(2,1)S(1)}, u32[]{:S(2)}, u32[]{:S(2)}) collective-permute-start(bf16[256,2048]{1,0:T(8,128)(2,1)S(1)} %rotated.19.refs_4_.refs_0_), channel_id=1, source_target_pairs={{0,1},{3,2},{4,5},{7,6},{8,9},{11,10},{12,13},{15,14},{16,17},{19,... | collective-permute-start | bytes 3145736 | tf_op jit(solution)/shard_map/ppermute | solution.py:291
  112.7 5.4 %collective-permute-done.14.refs_2_ = bf16[256,2048]{1,0:T(8,128)(2,1)S(1)} collective-permute-done((bf16[256,2048]{1,0:T(8,128)(2,1)S(1)}, bf16[256,2048]{1,0:T(8,128)(2,1)S(1)}, u32[]{:S(2)}, u32[]{:S(2)}) %collective-permute-start.14) | collective-permute-done | bytes 1048608 | tf_op jit(solution)/shard_map/ppermute | solution.py:291
  127.5 10.9 %collective-permute-done.8.refs_2_ = bf16[256,3072]{1,0:T(8,128)(2,1)S(1)} collective-permute-done((bf16[256,3072]{1,0:T(8,128)(2,1)S(1)}, bf16[256,3072]{1,0:T(8,128)(2,1)S(1)}, u32[]{:S(2)}, u32[]{:S(2)}) %collective-permute-start.8) | collective-permute-done | bytes 1572896 | tf_op jit(solution)/shard_map/ppermute | solution.py:118
  142.9 8.2 %collective-permute-start.21 = (bf16[256,2048]{1,0:T(8,128)(2,1)S(1)}, bf16[256,2048]{1,0:T(8,128)(2,1)}, u32[]{:S(2)}, u32[]{:S(2)}) collective-permute-start(bf16[256,2048]{1,0:T(8,128)(2,1)S(1)} %rotated.21.refs_3_.refs_0_.refs_4_), channel_id=1, source_target_pairs={{0,1},{3,2},{4,5},{7,6},{8,9},{11,10},{12,13},{15,14},{16,17},{19,... | collective-permute-start | bytes 3145736 | tf_op jit(solution)/shard_map/ppermute | solution.py:291
  159.5 3.7 products.11
  164.5 8.6 %collective-permute-done.21.refs_2_ = bf16[256,2048]{1,0:T(8,128)(2,1)} collective-permute-done((bf16[256,2048]{1,0:T(8,128)(2,1)S(1)}, bf16[256,2048]{1,0:T(8,128)(2,1)}, u32[]{:S(2)}, u32[]{:S(2)}) %collective-permute-start.21) | collective-permute-done | bytes 1048608 | tf_op jit(solution)/shard_map/ppermute | solution.py:291
  173.1 3.7 partial_grad.12.refs_2_.refs_0_
  185.9 6.8 %collective-permute-start.23 = (bf16[256,2048]{1,0:T(8,128)(2,1)S(1)}, bf16[256,2048]{1,0:T(8,128)(2,1)}, u32[]{:S(2)}, u32[]{:S(2)}) collective-permute-start(bf16[256,2048]{1,0:T(8,128)(2,1)S(1)} %rotated.23.refs_3_.refs_0_.refs_4_), channel_id=1, source_target_pairs={{0,1},{3,2},{4,5},{7,6},{8,9},{11,10},{12,13},{15,14},{16,17},{19,... | collective-permute-start | bytes 3145736 | tf_op jit(solution)/shard_map/ppermute | solution.py:291
  202.0 3.7 products.12
  205.7 7.8 %collective-permute-done.23.refs_2_ = bf16[256,2048]{1,0:T(8,128)(2,1)} collective-permute-done((bf16[256,2048]{1,0:T(8,128)(2,1)S(1)}, bf16[256,2048]{1,0:T(8,128)(2,1)}, u32[]{:S(2)}, u32[]{:S(2)}) %collective-permute-start.23) | collective-permute-done | bytes 1048608 | tf_op jit(solution)/shard_map/ppermute | solution.py:291
  221.5 4.7 %collective-permute-done.25.refs_2_ = bf16[256,4096]{1,0:T(8,128)(2,1)} collective-permute-done((bf16[256,4096]{1,0:T(8,128)(2,1)S(1)}, bf16[256,4096]{1,0:T(8,128)(2,1)}, u32[]{:S(2)}, u32[]{:S(2)}) %collective-permute-start.25) | collective-permute-done | bytes 2097184 | tf_op jit(solution)/shard_map/ppermute | solution.py:118
  228.2 8.4 %collective-permute-start.27 = (bf16[256,2048]{1,0:T(8,128)(2,1)S(1)}, bf16[256,2048]{1,0:T(8,128)(2,1)S(1)}, u32[]{:S(2)}, u32[]{:S(2)}) collective-permute-start(bf16[256,2048]{1,0:T(8,128)(2,1)S(1)} %rotated.25.refs_3_.refs_0_.refs_4_), channel_id=1, source_target_pairs={{0,1},{3,2},{4,5},{7,6},{8,9},{11,10},{12,13},{15,14},{16,17},{19,... | collective-permute-start | bytes 3145736 | tf_op jit(solution)/shard_map/ppermute | solution.py:291
  238.0 5.5 %collective-permute-done.29.refs_2_ = bf16[2048,512]{1,0:T(8,128)(2,1)} collective-permute-done((bf16[2048,512]{1,0:T(8,128)(2,1)}, bf16[2048,512]{1,0:T(8,128)(2,1)}, u32[]{:S(2)}, u32[]{:S(2)}) %collective-permute-start.29) | collective-permute-done | bytes 2097184 | tf_op jit(solution)/shard_map/ppermute | solution.py:311
  265.5 12.5 %collective-permute-done.22.refs_2_ = bf16[256,3072]{1,0:T(8,128)(2,1)} collective-permute-done((bf16[256,3072]{1,0:T(8,128)(2,1)S(1)}, bf16[256,3072]{1,0:T(8,128)(2,1)}, u32[]{:S(2)}, u32[]{:S(2)}) %collective-permute-start.22) | collective-permute-done | bytes 1572896 | tf_op jit(solution)/shard_map/ppermute | solution.py:118
  279.7 8.7 %collective-permute-done.31.refs_2_ = bf16[2048,512]{1,0:T(8,128)(2,1)} collective-permute-done((bf16[2048,512]{1,0:T(8,128)(2,1)S(1)}, bf16[2048,512]{1,0:T(8,128)(2,1)}, u32[]{:S(2)}, u32[]{:S(2)}) %collective-permute-start.31) | collective-permute-done | bytes 2097184 | tf_op jit(solution)/shard_map/ppermute | solution.py:311
  309.9 23.4 %collective-permute-done.33.refs_2_ = bf16[2048,512]{1,0:T(8,128)(2,1)} collective-permute-done((bf16[2048,512]{1,0:T(8,128)(2,1)}, bf16[2048,512]{1,0:T(8,128)(2,1)}, u32[]{:S(2)}, u32[]{:S(2)}) %collective-permute-start.33) | collective-permute-done | bytes 2097184 | tf_op jit(solution)/shard_map/ppermute | solution.py:311
  344.8 17.0 %collective-permute-done.39.refs_2_ = bf16[256,2048]{1,0:T(8,128)(2,1)S(1)} collective-permute-done((bf16[256,2048]{1,0:T(8,128)(2,1)S(1)}, bf16[256,2048]{1,0:T(8,128)(2,1)S(1)}, u32[]{:S(2)}, u32[]{:S(2)}) %collective-permute-start.39) | collective-permute-done | bytes 1048608 | tf_op jit(solution)/shard_map/ppermute | solution.py:118
  367.4 10.9 %collective-permute-done.41.refs_2_ = bf16[2048,512]{1,0:T(8,128)(2,1)} collective-permute-done((bf16[2048,512]{1,0:T(8,128)(2,1)S(1)}, bf16[2048,512]{1,0:T(8,128)(2,1)}, u32[]{:S(2)}, u32[]{:S(2)}) %collective-permute-start.41) | collective-permute-done | bytes 2097184 | tf_op jit(solution)/shard_map/ppermute | solution.py:311
  389.1 9.5 %collective-permute-done.44.refs_2_ = bf16[1024,512]{1,0:T(8,128)(2,1)} collective-permute-done((bf16[1024,512]{1,0:T(8,128)(2,1)S(1)}, bf16[1024,512]{1,0:T(8,128)(2,1)}, u32[]{:S(2)}, u32[]{:S(2)}) %collective-permute-start.44) | collective-permute-done | bytes 1048608 | tf_op jit(solution)/shard_map/ppermute | solution.py:311
  (190 shorter events, 207.6 us)
Async XLA Ops:
  0.6 43.7 %collective-permute-start = (bf16[13312,512]{1,0:T(8,128)(2,1)}, bf16[13312,512]{1,0:T(8,128)(2,1)}, u32[]{:S(2)}, u32[]{:S(2)}) collective-permute-start(bf16[13312,512]{1,0:T(8,128)(2,1)} %refs_2_.15), channel_id=1, source_target_pairs={{0,4},{4,0},{8,12},{12,8},{1,5},{5,1},{9,13},{13,9},{2,6},{6,2},{1... | collective-permute-start | bytes 40894472 | tf_op jit(solution)/shard_map/ppermute | solution.py:118
  47.3 45.7 %collective-permute-start.11 = (bf16[256,3072]{1,0:T(8,128)(2,1)}, bf16[256,3072]{1,0:T(8,128)(2,1)}, u32[]{:S(2)}, u32[]{:S(2)}) collective-permute-start(bf16[256,3072]{1,0:T(8,128)(2,1)} %get-tuple-element.20.refs_4_.refs_1_), channel_id=1, source_target_pairs={{0,8},{4,12},{8,0},{12,4},{1,9},{5,13},{9,1},{13,5},{2,10},{6,14},... | collective-permute-start | bytes 4718600 | tf_op jit(solution)/shard_map/ppermute | solution.py:118
  82.0 42.3 %collective-permute-start.10 = (bf16[2048,512]{1,0:T(8,128)(2,1)}, bf16[2048,512]{1,0:T(8,128)(2,1)}, u32[]{:S(2)}, u32[]{:S(2)}) collective-permute-start(bf16[2048,512]{1,0:T(8,128)(2,1)} %partial_grad.10.refs_3_.refs_0_), channel_id=1, source_target_pairs={{1,2},{2,1},{5,6},{6,5},{9,10},{10,9},{13,14},{14,13},{17,18},{18,... | collective-permute-start | bytes 6291464 | tf_op jit(solution)/shard_map/ppermute | solution.py:304
  101.0 37.4 %collective-permute-start.8 = (bf16[256,3072]{1,0:T(8,128)(2,1)S(1)}, bf16[256,3072]{1,0:T(8,128)(2,1)S(1)}, u32[]{:S(2)}, u32[]{:S(2)}) collective-permute-start(bf16[256,3072]{1,0:T(8,128)(2,1)S(1)} %get-tuple-element.21.refs_4_.refs_1_), channel_id=1, source_target_pairs={{0,8},{4,12},{8,0},{12,4},{1,9},{5,13},{9,1},{13,5},{2,10},{6,14},... | collective-permute-start | bytes 4718600 | tf_op jit(solution)/shard_map/ppermute | solution.py:118
  104.9 37.9 %collective-permute-start.16 = (bf16[1024,512]{1,0:T(8,128)(2,1)}, bf16[1024,512]{1,0:T(8,128)(2,1)}, u32[]{:S(2)}, u32[]{:S(2)}) collective-permute-start(bf16[1024,512]{1,0:T(8,128)(2,1)} %added.9.refs_4_.refs_1_), channel_id=1, source_target_pairs={{1,0},{2,3},{5,4},{6,7},{9,8},{10,11},{13,12},{14,15},{17,16},{18,... | collective-permute-start | bytes 3145736 | tf_op jit(solution)/shard_map/ppermute | solution.py:311
  120.8 58.0 %collective-permute-start.20 = (bf16[2048,512]{1,0:T(8,128)(2,1)}, bf16[2048,512]{1,0:T(8,128)(2,1)}, u32[]{:S(2)}, u32[]{:S(2)}) collective-permute-start(bf16[2048,512]{1,0:T(8,128)(2,1)} %partial_grad.11.refs_2_.refs_0_), channel_id=1, source_target_pairs={{1,2},{2,1},{5,6},{6,5},{9,10},{10,9},{13,14},{14,13},{17,18},{18,... | collective-permute-start | bytes 6291464 | tf_op jit(solution)/shard_map/ppermute | solution.py:304
  122.8 61.0 %collective-permute-start.17 = (bf16[256,4096]{1,0:T(8,128)(2,1)S(1)}, bf16[256,4096]{1,0:T(8,128)(2,1)}, u32[]{:S(2)}, u32[]{:S(2)}) collective-permute-start(bf16[256,4096]{1,0:T(8,128)(2,1)S(1)} %copy-done.2), channel_id=1, source_target_pairs={{0,8},{4,12},{8,0},{12,4},{1,9},{5,13},{9,1},{13,5},{2,10},{6,14},... | collective-permute-start | bytes 6291464 | tf_op jit(solution)/shard_map/ppermute | solution.py:118
  126.2 66.5 %collective-permute-start.19 = (bf16[2048,512]{1,0:T(8,128)(2,1)S(1)}, bf16[2048,512]{1,0:T(8,128)(2,1)}, u32[]{:S(2)}, u32[]{:S(2)}) collective-permute-start(bf16[2048,512]{1,0:T(8,128)(2,1)S(1)} %added.10.refs_4_.refs_1_), channel_id=1, source_target_pairs={{1,0},{2,3},{5,4},{6,7},{9,8},{10,11},{13,12},{14,15},{17,16},{18,... | collective-permute-start | bytes 6291464 | tf_op jit(solution)/shard_map/ppermute | solution.py:311
  158.0 37.7 %collective-permute-start.18 = (bf16[1024,512]{1,0:T(8,128)(2,1)}, bf16[1024,512]{1,0:T(8,128)(2,1)S(1)}, u32[]{:S(2)}, u32[]{:S(2)}) collective-permute-start(bf16[1024,512]{1,0:T(8,128)(2,1)} %chosen.9.refs_3_.refs_1_), channel_id=1, source_target_pairs={{0,4},{4,0},{8,12},{12,8},{1,5},{5,1},{9,13},{13,9},{2,6},{6,2},{1... | collective-permute-start | bytes 3145736 | tf_op jit(solution)/shard_map/ppermute | solution.py:118
  176.8 42.2 %collective-permute-start.26 = (bf16[2048,512]{1,0:T(8,128)(2,1)}, bf16[2048,512]{1,0:T(8,128)(2,1)}, u32[]{:S(2)}, u32[]{:S(2)}) collective-permute-start(bf16[2048,512]{1,0:T(8,128)(2,1)} %partial_grad.12.refs_2_.refs_0_), channel_id=1, source_target_pairs={{1,2},{2,1},{5,6},{6,5},{9,10},{10,9},{13,14},{14,13},{17,18},{18,... | collective-permute-start | bytes 6291464 | tf_op jit(solution)/shard_map/ppermute | solution.py:304
  178.8 47.4 %collective-permute-start.25 = (bf16[256,4096]{1,0:T(8,128)(2,1)S(1)}, bf16[256,4096]{1,0:T(8,128)(2,1)}, u32[]{:S(2)}, u32[]{:S(2)}) collective-permute-start(bf16[256,4096]{1,0:T(8,128)(2,1)S(1)} %copy-done.4), channel_id=1, source_target_pairs={{0,8},{4,12},{8,0},{12,4},{1,9},{5,13},{9,1},{13,5},{2,10},{6,14},... | collective-permute-start | bytes 6291464 | tf_op jit(solution)/shard_map/ppermute | solution.py:118
  192.7 50.8 %collective-permute-start.29 = (bf16[2048,512]{1,0:T(8,128)(2,1)}, bf16[2048,512]{1,0:T(8,128)(2,1)}, u32[]{:S(2)}, u32[]{:S(2)}) collective-permute-start(bf16[2048,512]{1,0:T(8,128)(2,1)} %added.11.refs_4_.refs_1_), channel_id=1, source_target_pairs={{1,0},{2,3},{5,4},{6,7},{9,8},{10,11},{13,12},{14,15},{17,16},{18,... | collective-permute-start | bytes 6291464 | tf_op jit(solution)/shard_map/ppermute | solution.py:311
  195.7 51.2 %collective-permute-start.28 = (bf16[2048,512]{1,0:T(8,128)(2,1)S(1)}, bf16[2048,512]{1,0:T(8,128)(2,1)}, u32[]{:S(2)}, u32[]{:S(2)}) collective-permute-start(bf16[2048,512]{1,0:T(8,128)(2,1)S(1)} %chosen.10.refs_4_.refs_1_), channel_id=1, source_target_pairs={{0,4},{4,0},{8,12},{12,8},{1,5},{5,1},{9,13},{13,9},{2,6},{6,2},{1... | collective-permute-start | bytes 6291464 | tf_op jit(solution)/shard_map/ppermute | solution.py:118
  217.0 44.3 %collective-permute-start.24 = (bf16[2048,512]{1,0:T(8,128)(2,1)}, bf16[2048,512]{1,0:T(8,128)(2,1)}, u32[]{:S(2)}, u32[]{:S(2)}) collective-permute-start(bf16[2048,512]{1,0:T(8,128)(2,1)} %partial_grad.13.refs_2_.refs_0_), channel_id=1, source_target_pairs={{1,2},{2,1},{5,6},{6,5},{9,10},{10,9},{13,14},{14,13},{17,18},{18,... | collective-permute-start | bytes 6291464 | tf_op jit(solution)/shard_map/ppermute | solution.py:304
  236.7 51.7 %collective-permute-start.31 = (bf16[2048,512]{1,0:T(8,128)(2,1)S(1)}, bf16[2048,512]{1,0:T(8,128)(2,1)}, u32[]{:S(2)}, u32[]{:S(2)}) collective-permute-start(bf16[2048,512]{1,0:T(8,128)(2,1)S(1)} %added.12.refs_4_.refs_1_), channel_id=1, source_target_pairs={{1,0},{2,3},{5,4},{6,7},{9,8},{10,11},{13,12},{14,15},{17,16},{18,... | collective-permute-start | bytes 6291464 | tf_op jit(solution)/shard_map/ppermute | solution.py:311
  243.5 34.6 %collective-permute-start.22 = (bf16[256,3072]{1,0:T(8,128)(2,1)S(1)}, bf16[256,3072]{1,0:T(8,128)(2,1)}, u32[]{:S(2)}, u32[]{:S(2)}) collective-permute-start(bf16[256,3072]{1,0:T(8,128)(2,1)S(1)} %get-tuple-element.27.refs_4_.refs_1_), channel_id=1, source_target_pairs={{0,8},{4,12},{8,0},{12,4},{1,9},{5,13},{9,1},{13,5},{2,10},{6,14},... | collective-permute-start | bytes 4718600 | tf_op jit(solution)/shard_map/ppermute | solution.py:118
  246.9 44.8 %collective-permute-start.30 = (bf16[2048,512]{1,0:T(8,128)(2,1)}, bf16[2048,512]{1,0:T(8,128)(2,1)}, u32[]{:S(2)}, u32[]{:S(2)}) collective-permute-start(bf16[2048,512]{1,0:T(8,128)(2,1)} %chosen.11.refs_4_.refs_1_), channel_id=1, source_target_pairs={{0,4},{4,0},{8,12},{12,8},{1,5},{5,1},{9,13},{13,9},{2,6},{6,2},{1... | collective-permute-start | bytes 6291464 | tf_op jit(solution)/shard_map/ppermute | solution.py:118
  259.4 46.5 %collective-permute-start.34 = (bf16[2048,512]{1,0:T(8,128)(2,1)}, bf16[2048,512]{1,0:T(8,128)(2,1)}, u32[]{:S(2)}, u32[]{:S(2)}) collective-permute-start(bf16[2048,512]{1,0:T(8,128)(2,1)} %partial_grad.14.refs_2_.refs_0_), channel_id=1, source_target_pairs={{1,2},{2,1},{5,6},{6,5},{9,10},{10,9},{13,14},{14,13},{17,18},{18,... | collective-permute-start | bytes 6291464 | tf_op jit(solution)/shard_map/ppermute | solution.py:304
  264.2 69.1 %collective-permute-start.33 = (bf16[2048,512]{1,0:T(8,128)(2,1)}, bf16[2048,512]{1,0:T(8,128)(2,1)}, u32[]{:S(2)}, u32[]{:S(2)}) collective-permute-start(bf16[2048,512]{1,0:T(8,128)(2,1)} %added.13.refs_4_.refs_1_), channel_id=1, source_target_pairs={{1,0},{2,3},{5,4},{6,7},{9,8},{10,11},{13,12},{14,15},{17,16},{18,... | collective-permute-start | bytes 6291464 | tf_op jit(solution)/shard_map/ppermute | solution.py:311
  291.7 46.1 %collective-permute-start.32 = (bf16[2048,512]{1,0:T(8,128)(2,1)S(1)}, bf16[2048,512]{1,0:T(8,128)(2,1)}, u32[]{:S(2)}, u32[]{:S(2)}) collective-permute-start(bf16[2048,512]{1,0:T(8,128)(2,1)S(1)} %chosen.12.refs_4_.refs_1_), channel_id=1, source_target_pairs={{0,4},{4,0},{8,12},{12,8},{1,5},{5,1},{9,13},{13,9},{2,6},{6,2},{1... | collective-permute-start | bytes 6291464 | tf_op jit(solution)/shard_map/ppermute | solution.py:118
  308.4 69.9 %collective-permute-start.41 = (bf16[2048,512]{1,0:T(8,128)(2,1)S(1)}, bf16[2048,512]{1,0:T(8,128)(2,1)}, u32[]{:S(2)}, u32[]{:S(2)}) collective-permute-start(bf16[2048,512]{1,0:T(8,128)(2,1)S(1)} %added.14.refs_3_.refs_1_), channel_id=1, source_target_pairs={{1,0},{2,3},{5,4},{6,7},{9,8},{10,11},{13,12},{14,15},{17,16},{18,... | collective-permute-start | bytes 6291464 | tf_op jit(solution)/shard_map/ppermute | solution.py:311
  335.7 44.4 %collective-permute-start.40 = (bf16[2048,512]{1,0:T(8,128)(2,1)S(1)}, bf16[2048,512]{1,0:T(8,128)(2,1)}, u32[]{:S(2)}, u32[]{:S(2)}) collective-permute-start(bf16[2048,512]{1,0:T(8,128)(2,1)S(1)} %chosen.13.refs_4_.refs_1_), channel_id=1, source_target_pairs={{0,4},{4,0},{8,12},{12,8},{1,5},{5,1},{9,13},{13,9},{2,6},{6,2},{1... | collective-permute-start | bytes 6291464 | tf_op jit(solution)/shard_map/ppermute | solution.py:118
  343.1 41.1 %collective-permute-start.38 = (bf16[256,1024]{1,0:T(8,128)(2,1)S(1)}, bf16[256,1024]{1,0:T(8,128)(2,1)}, u32[]{:S(2)}, u32[]{:S(2)}) collective-permute-start(bf16[256,1024]{1,0:T(8,128)(2,1)S(1)} %get-tuple-element.34.refs_5_.refs_1_), channel_id=1, source_target_pairs={{0,8},{4,12},{8,0},{12,4},{1,9},{5,13},{9,1},{13,5},{2,10},{6,14},... | collective-permute-start | bytes 1572872 | tf_op jit(solution)/shard_map/ppermute | solution.py:118
  366.0 32.6 %collective-permute-start.44 = (bf16[1024,512]{1,0:T(8,128)(2,1)S(1)}, bf16[1024,512]{1,0:T(8,128)(2,1)}, u32[]{:S(2)}, u32[]{:S(2)}) collective-permute-start(bf16[1024,512]{1,0:T(8,128)(2,1)S(1)} %added.15.refs_3_.refs_1_), channel_id=1, source_target_pairs={{1,0},{2,3},{5,4},{6,7},{9,8},{10,11},{13,12},{14,15},{17,16},{18,... | collective-permute-start | bytes 3145736 | tf_op jit(solution)/shard_map/ppermute | solution.py:311
  (49 other events, 699.1 us)

commit v4 on v3

--- a/solution.py
+++ b/solution.py
@@ -331,8 +331,8 @@
     mix(1)
     turn(1)
     send_partial(0)
+    send_partial(1)
     send(3)
-    send_partial(1)
     mix(2)
     turn(2)
     send_total(0)
@@ -344,8 +344,8 @@
     for r in range(3, n + LAG + 1):
         on(send, r + 1, n + LAG)
         on(send_partial, r - 1)
-        if r == 3:
-            choose(0)
+        if r < 5:
+            choose(r - 3)
         if r >= n:
             on(mix, r, n + LAG)
             on(turn_back, r - LAG)
@@ -355,7 +355,7 @@
         on(send_total, r - 2)
         on(mix, r)
         on(turn, r)
-        if r > 3:
+        if r > 4:
             on(choose, r - 3)
         on(place_grad, r - 4)
         if r < n:

time: 407 us -> 403 us (level)
  Pallas kernels: 146 us -> 138 us
  waiting for transfers between devices: 158 us -> 163 us
    pallas_call x66, Pallas kernels: 146 us -> 138 us  [__call__(): pl.pallas_call(kernel, grid=(groups,), name=name, in_specs=specs, out_spe...]
    ppermute x8, waiting for transfers between devices: 40.3 us -> 46 us  [turn(): outer[r] = lax.ppermute(rotated[r], 'dp', [(0, 1), (last, last - 1)])]
    unnamed x52 -> x54, local copies, waits for them, and re-layouts: 10.5 us -> 11.9 us
  transfers between devices with their start and end apart: 47 -> 47, of which waited for: 22 -> 22; matrix products, arithmetic and copies ran while one was open for 0% -> 0% of each run, Pallas kernels for 36% -> 34%
where the time goes in v4:
time: 403 us; the launch traced here: 401 us
  waiting for transfers between devices  163 us (40%)
  Pallas kernels  138 us (34%)
  starting transfers between devices  86.3 us (21%)
  local copies, waits for them, and re-layouts  11.9 us (3%)
    pallas_call x66, Pallas kernels, __call__(): pl.pallas_call(kernel, grid=(groups,), name=name, in_specs=specs, out_spe...  138 us
    ppermute x8, waiting for transfers between devices, send_total(): lax.ppermute(moving, 'dp', [(step, step - 1), (last - step, last - step +...  62.1 us
    ppermute x22, waiting for transfers between devices, swap(): return lax.ppermute(array, 'tensor', pairs)  51.3 us
    ppermute x8, waiting for transfers between devices, turn(): outer[r] = lax.ppermute(rotated[r], 'dp', [(0, 1), (last, last - 1)])  46 us
    ppermute x8, starting transfers between devices, turn(): outer[r] = lax.ppermute(rotated[r], 'dp', [(0, 1), (last, last - 1)])  45.6 us
    ppermute x22, starting transfers between devices, swap(): return lax.ppermute(array, 'tensor', pairs)  13.4 us
    ppermute x8, starting transfers between devices, send_partial(): other[j] = lax.ppermute(mine[j], 'dp', [(half - 1, half), (half, half - 1)])  13.3 us
    unnamed x54, local copies, waits for them, and re-layouts  11.9 us
  transfers between devices with their start and end apart: 47, of which 22 were waited for; matrix products, arithmetic and copies ran while one was open for 0% of the time, Pallas kernels for 34%

profile of v4, /device:TPU:0, one launch (start us, length us, event | category | flops | bytes accessed | tf_op | source)
XLA Modules:
  0.0 401.3 jit_solution(14655271681697445661)
XLA Ops:
  10.3 3.9 collective-permute-done.3.refs_5_.refs_3_
  19.0 4.0 collective-permute-start.5
  30.2 4.0 collective-permute-start.4
  35.7 9.1 %collective-permute-done.4.refs_2_ = bf16[256,1024]{1,0:T(8,128)(2,1)S(1)} collective-permute-done((bf16[256,1024]{1,0:T(8,128)(2,1)S(1)}, bf16[256,1024]{1,0:T(8,128)(2,1)S(1)}, u32[]{:S(2)}, u32[]{:S(2)}) %collective-permute-start.4) | collective-permute-done | bytes 524320 | tf_op jit(solution)/shard_map/ppermute | solution.py:291
  55.0 4.5 %collective-permute-start.9 = (bf16[256,2048]{1,0:T(8,128)(2,1)S(1)}, bf16[256,2048]{1,0:T(8,128)(2,1)S(1)}, u32[]{:S(2)}, u32[]{:S(2)}) collective-permute-start(bf16[256,2048]{1,0:T(8,128)(2,1)S(1)} %rotated.18.refs_2_.refs_0_.refs_4_), channel_id=1, source_target_pairs={{0,1},{3,2},{4,5},{7,6},{8,9},{11,10},{12,13},{15,14},{16,17},{19,... | collective-permute-start | bytes 3145736 | tf_op jit(solution)/shard_map/ppermute | solution.py:291
  67.4 12.6 %collective-permute-done.9.refs_2_ = bf16[256,2048]{1,0:T(8,128)(2,1)S(1)} collective-permute-done((bf16[256,2048]{1,0:T(8,128)(2,1)S(1)}, bf16[256,2048]{1,0:T(8,128)(2,1)S(1)}, u32[]{:S(2)}, u32[]{:S(2)}) %collective-permute-start.9) | collective-permute-done | bytes 1048608 | tf_op jit(solution)/shard_map/ppermute | solution.py:291
  93.1 6.6 %collective-permute-start.15 = (bf16[256,2048]{1,0:T(8,128)(2,1)S(1)}, bf16[256,2048]{1,0:T(8,128)(2,1)S(1)}, u32[]{:S(2)}, u32[]{:S(2)}) collective-permute-start(bf16[256,2048]{1,0:T(8,128)(2,1)S(1)} %rotated.19.refs_4_.refs_0_), channel_id=1, source_target_pairs={{0,1},{3,2},{4,5},{7,6},{8,9},{11,10},{12,13},{15,14},{16,17},{19,... | collective-permute-start | bytes 3145736 | tf_op jit(solution)/shard_map/ppermute | solution.py:291
  111.6 5.7 %collective-permute-done.15.refs_2_ = bf16[256,2048]{1,0:T(8,128)(2,1)S(1)} collective-permute-done((bf16[256,2048]{1,0:T(8,128)(2,1)S(1)}, bf16[256,2048]{1,0:T(8,128)(2,1)S(1)}, u32[]{:S(2)}, u32[]{:S(2)}) %collective-permute-start.15) | collective-permute-done | bytes 1048608 | tf_op jit(solution)/shard_map/ppermute | solution.py:291
  127.1 10.1 %collective-permute-done.8.refs_2_ = bf16[256,3072]{1,0:T(8,128)(2,1)} collective-permute-done((bf16[256,3072]{1,0:T(8,128)(2,1)S(1)}, bf16[256,3072]{1,0:T(8,128)(2,1)}, u32[]{:S(2)}, u32[]{:S(2)}) %collective-permute-start.8) | collective-permute-done | bytes 1572896 | tf_op jit(solution)/shard_map/ppermute | solution.py:118
  139.2 9.2 %collective-permute-start.21 = (bf16[256,2048]{1,0:T(8,128)(2,1)S(1)}, bf16[256,2048]{1,0:T(8,128)(2,1)S(1)}, u32[]{:S(2)}, u32[]{:S(2)}) collective-permute-start(bf16[256,2048]{1,0:T(8,128)(2,1)S(1)} %rotated.21.refs_3_.refs_0_.refs_4_), channel_id=1, source_target_pairs={{0,1},{3,2},{4,5},{7,6},{8,9},{11,10},{12,13},{15,14},{16,17},{19,... | collective-permute-start | bytes 3145736 | tf_op jit(solution)/shard_map/ppermute | solution.py:291
  159.0 12.2 %collective-permute-done.21.refs_2_ = bf16[256,2048]{1,0:T(8,128)(2,1)S(1)} collective-permute-done((bf16[256,2048]{1,0:T(8,128)(2,1)S(1)}, bf16[256,2048]{1,0:T(8,128)(2,1)S(1)}, u32[]{:S(2)}, u32[]{:S(2)}) %collective-permute-start.21) | collective-permute-done | bytes 1048608 | tf_op jit(solution)/shard_map/ppermute | solution.py:291
  181.6 8.5 %collective-permute-start.23 = (bf16[256,2048]{1,0:T(8,128)(2,1)S(1)}, bf16[256,2048]{1,0:T(8,128)(2,1)}, u32[]{:S(2)}, u32[]{:S(2)}) collective-permute-start(bf16[256,2048]{1,0:T(8,128)(2,1)S(1)} %rotated.23.refs_3_.refs_0_.refs_4_), channel_id=1, source_target_pairs={{0,1},{3,2},{4,5},{7,6},{8,9},{11,10},{12,13},{15,14},{16,17},{19,... | collective-permute-start | bytes 3145736 | tf_op jit(solution)/shard_map/ppermute | solution.py:291
  203.9 5.4 %collective-permute-done.23.refs_2_ = bf16[256,2048]{1,0:T(8,128)(2,1)} collective-permute-done((bf16[256,2048]{1,0:T(8,128)(2,1)S(1)}, bf16[256,2048]{1,0:T(8,128)(2,1)}, u32[]{:S(2)}, u32[]{:S(2)}) %collective-permute-start.23) | collective-permute-done | bytes 1048608 | tf_op jit(solution)/shard_map/ppermute | solution.py:291
  209.3 3.7 partial_grad.13.refs_2_.refs_0_
  216.9 5.4 %collective-permute-done.25.refs_2_ = bf16[256,4096]{1,0:T(8,128)(2,1)} collective-permute-done((bf16[256,4096]{1,0:T(8,128)(2,1)S(1)}, bf16[256,4096]{1,0:T(8,128)(2,1)}, u32[]{:S(2)}, u32[]{:S(2)}) %collective-permute-start.25) | collective-permute-done | bytes 2097184 | tf_op jit(solution)/shard_map/ppermute | solution.py:118
  224.4 7.5 %collective-permute-start.27 = (bf16[256,2048]{1,0:T(8,128)(2,1)S(1)}, bf16[256,2048]{1,0:T(8,128)(2,1)S(1)}, u32[]{:S(2)}, u32[]{:S(2)}) collective-permute-start(bf16[256,2048]{1,0:T(8,128)(2,1)S(1)} %rotated.25.refs_3_.refs_0_.refs_4_), channel_id=1, source_target_pairs={{0,1},{3,2},{4,5},{7,6},{8,9},{11,10},{12,13},{15,14},{16,17},{19,... | collective-permute-start | bytes 3145736 | tf_op jit(solution)/shard_map/ppermute | solution.py:291
  233.1 6.0 %collective-permute-done.29.refs_2_ = bf16[2048,512]{1,0:T(8,128)(2,1)} collective-permute-done((bf16[2048,512]{1,0:T(8,128)(2,1)}, bf16[2048,512]{1,0:T(8,128)(2,1)}, u32[]{:S(2)}, u32[]{:S(2)}) %collective-permute-start.29) | collective-permute-done | bytes 2097184 | tf_op jit(solution)/shard_map/ppermute | solution.py:311
  248.4 4.0 products.13
  264.3 9.2 %collective-permute-done.22.refs_2_ = bf16[256,3072]{1,0:T(8,128)(2,1)} collective-permute-done((bf16[256,3072]{1,0:T(8,128)(2,1)S(1)}, bf16[256,3072]{1,0:T(8,128)(2,1)}, u32[]{:S(2)}, u32[]{:S(2)}) %collective-permute-start.22) | collective-permute-done | bytes 1572896 | tf_op jit(solution)/shard_map/ppermute | solution.py:118
  275.1 9.0 %collective-permute-done.31.refs_2_ = bf16[2048,512]{1,0:T(8,128)(2,1)} collective-permute-done((bf16[2048,512]{1,0:T(8,128)(2,1)S(1)}, bf16[2048,512]{1,0:T(8,128)(2,1)}, u32[]{:S(2)}, u32[]{:S(2)}) %collective-permute-start.31) | collective-permute-done | bytes 2097184 | tf_op jit(solution)/shard_map/ppermute | solution.py:311
  306.2 22.9 %collective-permute-done.33.refs_2_ = bf16[2048,512]{1,0:T(8,128)(2,1)} collective-permute-done((bf16[2048,512]{1,0:T(8,128)(2,1)}, bf16[2048,512]{1,0:T(8,128)(2,1)}, u32[]{:S(2)}, u32[]{:S(2)}) %collective-permute-start.33) | collective-permute-done | bytes 2097184 | tf_op jit(solution)/shard_map/ppermute | solution.py:311
  339.6 17.9 %collective-permute-done.39.refs_2_ = bf16[256,2048]{1,0:T(8,128)(2,1)S(1)} collective-permute-done((bf16[256,2048]{1,0:T(8,128)(2,1)S(1)}, bf16[256,2048]{1,0:T(8,128)(2,1)S(1)}, u32[]{:S(2)}, u32[]{:S(2)}) %collective-permute-start.39) | collective-permute-done | bytes 1048608 | tf_op jit(solution)/shard_map/ppermute | solution.py:118
  361.5 12.5 %collective-permute-done.41.refs_2_ = bf16[2048,512]{1,0:T(8,128)(2,1)} collective-permute-done((bf16[2048,512]{1,0:T(8,128)(2,1)}, bf16[2048,512]{1,0:T(8,128)(2,1)}, u32[]{:S(2)}, u32[]{:S(2)}) %collective-permute-start.41) | collective-permute-done | bytes 2097184 | tf_op jit(solution)/shard_map/ppermute | solution.py:311
  384.3 10.2 %collective-permute-done.44.refs_2_ = bf16[1024,512]{1,0:T(8,128)(2,1)} collective-permute-done((bf16[1024,512]{1,0:T(8,128)(2,1)S(1)}, bf16[1024,512]{1,0:T(8,128)(2,1)}, u32[]{:S(2)}, u32[]{:S(2)}) %collective-permute-start.44) | collective-permute-done | bytes 1048608 | tf_op jit(solution)/shard_map/ppermute | solution.py:311
  (192 shorter events, 196.0 us)
Async XLA Ops:
  0.6 48.0 %collective-permute-start = (bf16[13312,512]{1,0:T(8,128)(2,1)}, bf16[13312,512]{1,0:T(8,128)(2,1)}, u32[]{:S(2)}, u32[]{:S(2)}) collective-permute-start(bf16[13312,512]{1,0:T(8,128)(2,1)} %refs_2_.15), channel_id=1, source_target_pairs={{0,4},{4,0},{8,12},{12,8},{1,5},{5,1},{9,13},{13,9},{2,6},{6,2},{1... | collective-permute-start | bytes 40894472 | tf_op jit(solution)/shard_map/ppermute | solution.py:118
  51.6 39.4 %collective-permute-start.14 = (bf16[256,3072]{1,0:T(8,128)(2,1)}, bf16[256,3072]{1,0:T(8,128)(2,1)}, u32[]{:S(2)}, u32[]{:S(2)}) collective-permute-start(bf16[256,3072]{1,0:T(8,128)(2,1)} %get-tuple-element.20.refs_4_.refs_1_), channel_id=1, source_target_pairs={{0,8},{4,12},{8,0},{12,4},{1,9},{5,13},{9,1},{13,5},{2,10},{6,14},... | collective-permute-start | bytes 4718600 | tf_op jit(solution)/shard_map/ppermute | solution.py:118
  82.7 40.3 %collective-permute-start.10 = (bf16[2048,512]{1,0:T(8,128)(2,1)}, bf16[2048,512]{1,0:T(8,128)(2,1)}, u32[]{:S(2)}, u32[]{:S(2)}) collective-permute-start(bf16[2048,512]{1,0:T(8,128)(2,1)} %partial_grad.10.refs_3_.refs_0_), channel_id=1, source_target_pairs={{1,2},{2,1},{5,6},{6,5},{9,10},{10,9},{13,14},{14,13},{17,18},{18,... | collective-permute-start | bytes 6291464 | tf_op jit(solution)/shard_map/ppermute | solution.py:304
  99.7 37.5 %collective-permute-start.8 = (bf16[256,3072]{1,0:T(8,128)(2,1)S(1)}, bf16[256,3072]{1,0:T(8,128)(2,1)}, u32[]{:S(2)}, u32[]{:S(2)}) collective-permute-start(bf16[256,3072]{1,0:T(8,128)(2,1)S(1)} %get-tuple-element.21.refs_4_.refs_1_), channel_id=1, source_target_pairs={{0,8},{4,12},{8,0},{12,4},{1,9},{5,13},{9,1},{13,5},{2,10},{6,14},... | collective-permute-start | bytes 4718600 | tf_op jit(solution)/shard_map/ppermute | solution.py:118
  119.0 56.0 %collective-permute-start.20 = (bf16[2048,512]{1,0:T(8,128)(2,1)S(1)}, bf16[2048,512]{1,0:T(8,128)(2,1)}, u32[]{:S(2)}, u32[]{:S(2)}) collective-permute-start(bf16[2048,512]{1,0:T(8,128)(2,1)S(1)} %partial_grad.11.refs_3_.refs_0_), channel_id=1, source_target_pairs={{1,2},{2,1},{5,6},{6,5},{9,10},{10,9},{13,14},{14,13},{17,18},{18,... | collective-permute-start | bytes 6291464 | tf_op jit(solution)/shard_map/ppermute | solution.py:304
  121.2 58.4 %collective-permute-start.17 = (bf16[256,4096]{1,0:T(8,128)(2,1)S(1)}, bf16[256,4096]{1,0:T(8,128)(2,1)}, u32[]{:S(2)}, u32[]{:S(2)}) collective-permute-start(bf16[256,4096]{1,0:T(8,128)(2,1)S(1)} %copy-done.2), channel_id=1, source_target_pairs={{0,8},{4,12},{8,0},{12,4},{1,9},{5,13},{9,1},{13,5},{2,10},{6,14},... | collective-permute-start | bytes 6291464 | tf_op jit(solution)/shard_map/ppermute | solution.py:118
  125.7 64.3 %collective-permute-start.19 = (bf16[2048,512]{1,0:T(8,128)(2,1)}, bf16[2048,512]{1,0:T(8,128)(2,1)}, u32[]{:S(2)}, u32[]{:S(2)}) collective-permute-start(bf16[2048,512]{1,0:T(8,128)(2,1)} %added.10.refs_4_.refs_1_), channel_id=1, source_target_pairs={{1,0},{2,3},{5,4},{6,7},{9,8},{10,11},{13,12},{14,15},{17,16},{18,... | collective-permute-start | bytes 6291464 | tf_op jit(solution)/shard_map/ppermute | solution.py:311
  139.2 32.0 %collective-permute-start.21 = (bf16[256,2048]{1,0:T(8,128)(2,1)S(1)}, bf16[256,2048]{1,0:T(8,128)(2,1)S(1)}, u32[]{:S(2)}, u32[]{:S(2)}) collective-permute-start(bf16[256,2048]{1,0:T(8,128)(2,1)S(1)} %rotated.21.refs_3_.refs_0_.refs_4_), channel_id=1, source_target_pairs={{0,1},{3,2},{4,5},{7,6},{8,9},{11,10},{12,13},{15,14},{16,17},{19,... | collective-permute-start | bytes 3145736 | tf_op jit(solution)/shard_map/ppermute | solution.py:291
  152.4 41.3 %collective-permute-start.18 = (bf16[1024,512]{1,0:T(8,128)(2,1)}, bf16[1024,512]{1,0:T(8,128)(2,1)S(1)}, u32[]{:S(2)}, u32[]{:S(2)}) collective-permute-start(bf16[1024,512]{1,0:T(8,128)(2,1)} %chosen.9.refs_2_.refs_1_), channel_id=1, source_target_pairs={{0,4},{4,0},{8,12},{12,8},{1,5},{5,1},{9,13},{13,9},{2,6},{6,2},{1... | collective-permute-start | bytes 3145736 | tf_op jit(solution)/shard_map/ppermute | solution.py:118
  172.9 42.2 %collective-permute-start.26 = (bf16[2048,512]{1,0:T(8,128)(2,1)S(1)}, bf16[2048,512]{1,0:T(8,128)(2,1)}, u32[]{:S(2)}, u32[]{:S(2)}) collective-permute-start(bf16[2048,512]{1,0:T(8,128)(2,1)S(1)} %partial_grad.12.refs_2_.refs_0_), channel_id=1, source_target_pairs={{1,2},{2,1},{5,6},{6,5},{9,10},{10,9},{13,14},{14,13},{17,18},{18,... | collective-permute-start | bytes 6291464 | tf_op jit(solution)/shard_map/ppermute | solution.py:304
  175.0 47.4 %collective-permute-start.25 = (bf16[256,4096]{1,0:T(8,128)(2,1)S(1)}, bf16[256,4096]{1,0:T(8,128)(2,1)}, u32[]{:S(2)}, u32[]{:S(2)}) collective-permute-start(bf16[256,4096]{1,0:T(8,128)(2,1)S(1)} %copy-done.4), channel_id=1, source_target_pairs={{0,8},{4,12},{8,0},{12,4},{1,9},{5,13},{9,1},{13,5},{2,10},{6,14},... | collective-permute-start | bytes 6291464 | tf_op jit(solution)/shard_map/ppermute | solution.py:118
  190.1 49.1 %collective-permute-start.29 = (bf16[2048,512]{1,0:T(8,128)(2,1)}, bf16[2048,512]{1,0:T(8,128)(2,1)}, u32[]{:S(2)}, u32[]{:S(2)}) collective-permute-start(bf16[2048,512]{1,0:T(8,128)(2,1)} %added.11.refs_4_.refs_1_), channel_id=1, source_target_pairs={{1,0},{2,3},{5,4},{6,7},{9,8},{10,11},{13,12},{14,15},{17,16},{18,... | collective-permute-start | bytes 6291464 | tf_op jit(solution)/shard_map/ppermute | solution.py:311
  193.7 47.8 %collective-permute-start.28 = (bf16[2048,512]{1,0:T(8,128)(2,1)S(1)}, bf16[2048,512]{1,0:T(8,128)(2,1)}, u32[]{:S(2)}, u32[]{:S(2)}) collective-permute-start(bf16[2048,512]{1,0:T(8,128)(2,1)S(1)} %chosen.10.refs_4_.refs_1_), channel_id=1, source_target_pairs={{0,4},{4,0},{8,12},{12,8},{1,5},{5,1},{9,13},{13,9},{2,6},{6,2},{1... | collective-permute-start | bytes 6291464 | tf_op jit(solution)/shard_map/ppermute | solution.py:118
  213.0 47.1 %collective-permute-start.24 = (bf16[2048,512]{1,0:T(8,128)(2,1)}, bf16[2048,512]{1,0:T(8,128)(2,1)}, u32[]{:S(2)}, u32[]{:S(2)}) collective-permute-start(bf16[2048,512]{1,0:T(8,128)(2,1)} %partial_grad.13.refs_2_.refs_0_), channel_id=1, source_target_pairs={{1,2},{2,1},{5,6},{6,5},{9,10},{10,9},{13,14},{14,13},{17,18},{18,... | collective-permute-start | bytes 6291464 | tf_op jit(solution)/shard_map/ppermute | solution.py:304
  231.8 52.3 %collective-permute-start.31 = (bf16[2048,512]{1,0:T(8,128)(2,1)S(1)}, bf16[2048,512]{1,0:T(8,128)(2,1)}, u32[]{:S(2)}, u32[]{:S(2)}) collective-permute-start(bf16[2048,512]{1,0:T(8,128)(2,1)S(1)} %added.12.refs_4_.refs_1_), channel_id=1, source_target_pairs={{1,0},{2,3},{5,4},{6,7},{9,8},{10,11},{13,12},{14,15},{17,16},{18,... | collective-permute-start | bytes 6291464 | tf_op jit(solution)/shard_map/ppermute | solution.py:311
  239.2 34.3 %collective-permute-start.22 = (bf16[256,3072]{1,0:T(8,128)(2,1)S(1)}, bf16[256,3072]{1,0:T(8,128)(2,1)}, u32[]{:S(2)}, u32[]{:S(2)}) collective-permute-start(bf16[256,3072]{1,0:T(8,128)(2,1)S(1)} %get-tuple-element.27.refs_4_.refs_1_), channel_id=1, source_target_pairs={{0,8},{4,12},{8,0},{12,4},{1,9},{5,13},{9,1},{13,5},{2,10},{6,14},... | collective-permute-start | bytes 4718600 | tf_op jit(solution)/shard_map/ppermute | solution.py:118
  241.5 45.9 %collective-permute-start.30 = (bf16[2048,512]{1,0:T(8,128)(2,1)S(1)}, bf16[2048,512]{1,0:T(8,128)(2,1)}, u32[]{:S(2)}, u32[]{:S(2)}) collective-permute-start(bf16[2048,512]{1,0:T(8,128)(2,1)S(1)} %chosen.11.refs_4_.refs_1_), channel_id=1, source_target_pairs={{0,4},{4,0},{8,12},{12,8},{1,5},{5,1},{9,13},{13,9},{2,6},{6,2},{1... | collective-permute-start | bytes 6291464 | tf_op jit(solution)/shard_map/ppermute | solution.py:118
  258.2 43.1 %collective-permute-start.34 = (bf16[2048,512]{1,0:T(8,128)(2,1)}, bf16[2048,512]{1,0:T(8,128)(2,1)}, u32[]{:S(2)}, u32[]{:S(2)}) collective-permute-start(bf16[2048,512]{1,0:T(8,128)(2,1)} %partial_grad.14.refs_2_.refs_0_), channel_id=1, source_target_pairs={{1,2},{2,1},{5,6},{6,5},{9,10},{10,9},{13,14},{14,13},{17,18},{18,... | collective-permute-start | bytes 6291464 | tf_op jit(solution)/shard_map/ppermute | solution.py:304
  263.0 66.1 %collective-permute-start.33 = (bf16[2048,512]{1,0:T(8,128)(2,1)}, bf16[2048,512]{1,0:T(8,128)(2,1)}, u32[]{:S(2)}, u32[]{:S(2)}) collective-permute-start(bf16[2048,512]{1,0:T(8,128)(2,1)} %added.13.refs_4_.refs_1_), channel_id=1, source_target_pairs={{1,0},{2,3},{5,4},{6,7},{9,8},{10,11},{13,12},{14,15},{17,16},{18,... | collective-permute-start | bytes 6291464 | tf_op jit(solution)/shard_map/ppermute | solution.py:311
  287.4 44.9 %collective-permute-start.32 = (bf16[2048,512]{1,0:T(8,128)(2,1)S(1)}, bf16[2048,512]{1,0:T(8,128)(2,1)}, u32[]{:S(2)}, u32[]{:S(2)}) collective-permute-start(bf16[2048,512]{1,0:T(8,128)(2,1)S(1)} %chosen.12.refs_4_.refs_1_), channel_id=1, source_target_pairs={{0,4},{4,0},{8,12},{12,8},{1,5},{5,1},{9,13},{13,9},{2,6},{6,2},{1... | collective-permute-start | bytes 6291464 | tf_op jit(solution)/shard_map/ppermute | solution.py:118
  304.8 69.3 %collective-permute-start.41 = (bf16[2048,512]{1,0:T(8,128)(2,1)}, bf16[2048,512]{1,0:T(8,128)(2,1)}, u32[]{:S(2)}, u32[]{:S(2)}) collective-permute-start(bf16[2048,512]{1,0:T(8,128)(2,1)} %added.14.refs_3_.refs_1_), channel_id=1, source_target_pairs={{1,0},{2,3},{5,4},{6,7},{9,8},{10,11},{13,12},{14,15},{17,16},{18,... | collective-permute-start | bytes 6291464 | tf_op jit(solution)/shard_map/ppermute | solution.py:311
  331.4 45.0 %collective-permute-start.40 = (bf16[2048,512]{1,0:T(8,128)(2,1)S(1)}, bf16[2048,512]{1,0:T(8,128)(2,1)S(1)}, u32[]{:S(2)}, u32[]{:S(2)}) collective-permute-start(bf16[2048,512]{1,0:T(8,128)(2,1)S(1)} %chosen.13.refs_4_.refs_1_), channel_id=1, source_target_pairs={{0,4},{4,0},{8,12},{12,8},{1,5},{5,1},{9,13},{13,9},{2,6},{6,2},{1... | collective-permute-start | bytes 6291464 | tf_op jit(solution)/shard_map/ppermute | solution.py:118
  337.9 41.9 %collective-permute-start.38 = (bf16[256,1024]{1,0:T(8,128)(2,1)S(1)}, bf16[256,1024]{1,0:T(8,128)(2,1)S(1)}, u32[]{:S(2)}, u32[]{:S(2)}) collective-permute-start(bf16[256,1024]{1,0:T(8,128)(2,1)S(1)} %get-tuple-element.34.refs_5_.refs_1_), channel_id=1, source_target_pairs={{0,8},{4,12},{8,0},{12,4},{1,9},{5,13},{9,1},{13,5},{2,10},{6,14},... | collective-permute-start | bytes 1572872 | tf_op jit(solution)/shard_map/ppermute | solution.py:118
  360.0 34.5 %collective-permute-start.44 = (bf16[1024,512]{1,0:T(8,128)(2,1)S(1)}, bf16[1024,512]{1,0:T(8,128)(2,1)}, u32[]{:S(2)}, u32[]{:S(2)}) collective-permute-start(bf16[1024,512]{1,0:T(8,128)(2,1)S(1)} %added.15.refs_3_.refs_1_), channel_id=1, source_target_pairs={{1,0},{2,3},{5,4},{6,7},{9,8},{10,11},{13,12},{14,15},{17,16},{18,... | collective-permute-start | bytes 3145736 | tf_op jit(solution)/shard_map/ppermute | solution.py:311
  (50 other events, 677.1 us)

commit v5 on v4

--- a/solution.py
+++ b/solution.py
@@ -104,6 +104,9 @@
     def grad_rows(first=0):
         return pl.BlockSpec(grad_block, lambda g: (first + g, 0))
 
+    def grad_halves():
+        return pl.BlockSpec((unit // 2, features), lambda g: (g, 0))
+
     def whole(array):
         return pl.BlockSpec(array.shape, lambda g: (0,) * array.ndim)
 
@@ -177,8 +180,8 @@
         def body(a_ref, b_ref, o_ref):
             o_ref[...] = ((a_ref[...].astype(F32) + b_ref[...].astype(F32)) * factor).astype(BF)
         return chain(
-            "added", body, CHUNKS[j], [(mine, grad_rows()), (other, grad_rows())],
-            [(grad_shape(j), grad_rows())],
+            "added", body, 2 * CHUNKS[j], [(mine, grad_halves()), (other, grad_halves())],
+            [(grad_shape(j), grad_halves())],
         )[0]
 
     def chosen(total, inners, j):

time: 403 us -> 406 us (level)
  Pallas kernels: 138 us -> 143 us
    pallas_call x66, Pallas kernels: 138 us -> 143 us  [__call__(): pl.pallas_call(kernel, grid=(groups,), name=name, in_specs=specs, out_spe...]
    ppermute x22, waiting for transfers between devices: 51.3 us -> 47.2 us  [swap(): return lax.ppermute(array, 'tensor', pairs)]
  transfers between devices with their start and end apart: 47 -> 47, of which waited for: 22 -> 21; matrix products, arithmetic and copies ran while one was open for 0% -> 0% of each run, Pallas kernels for 34% -> 35%
where the time goes in v5:
time: 406 us; the launch traced here: 404 us
  waiting for transfers between devices  159 us (39%)
  Pallas kernels  143 us (35%)
  starting transfers between devices  88.3 us (22%)
  local copies, waits for them, and re-layouts  11.5 us (3%)
    pallas_call x66, Pallas kernels, __call__(): pl.pallas_call(kernel, grid=(groups,), name=name, in_specs=specs, out_spe...  143 us
    ppermute x8, waiting for transfers between devices, send_total(): lax.ppermute(moving, 'dp', [(step, step - 1), (last - step, last - step +...  61 us
    ppermute x22, waiting for transfers between devices, swap(): return lax.ppermute(array, 'tensor', pairs)  47.2 us
    ppermute x8, waiting for transfers between devices, turn(): outer[r] = lax.ppermute(rotated[r], 'dp', [(0, 1), (last, last - 1)])  46.9 us
    ppermute x8, starting transfers between devices, turn(): outer[r] = lax.ppermute(rotated[r], 'dp', [(0, 1), (last, last - 1)])  45.9 us
    ppermute x22, starting transfers between devices, swap(): return lax.ppermute(array, 'tensor', pairs)  15.2 us
    ppermute x8, starting transfers between devices, send_partial(): other[j] = lax.ppermute(mine[j], 'dp', [(half - 1, half), (half, half - 1)])  13.3 us
    unnamed x54, local copies, waits for them, and re-layouts  11.5 us
  transfers between devices with their start and end apart: 47, of which 21 were waited for; matrix products, arithmetic and copies ran while one was open for 0% of the time, Pallas kernels for 35%

profile of v5, /device:TPU:0, one launch (start us, length us, event | category | flops | bytes accessed | tf_op | source)
XLA Modules:
  0.0 403.5 jit_solution(8991540551225239123)
XLA Ops:
  30.2 4.0 collective-permute-start.4
  35.7 9.1 %collective-permute-done.4.refs_2_ = bf16[256,1024]{1,0:T(8,128)(2,1)S(1)} collective-permute-done((bf16[256,1024]{1,0:T(8,128)(2,1)S(1)}, bf16[256,1024]{1,0:T(8,128)(2,1)S(1)}, u32[]{:S(2)}, u32[]{:S(2)}) %collective-permute-start.4) | collective-permute-done | bytes 524320 | tf_op jit(solution)/shard_map/ppermute | solution.py:294
  55.0 4.5 %collective-permute-start.9 = (bf16[256,2048]{1,0:T(8,128)(2,1)S(1)}, bf16[256,2048]{1,0:T(8,128)(2,1)S(1)}, u32[]{:S(2)}, u32[]{:S(2)}) collective-permute-start(bf16[256,2048]{1,0:T(8,128)(2,1)S(1)} %rotated.18.refs_2_.refs_0_.refs_4_), channel_id=1, source_target_pairs={{0,1},{3,2},{4,5},{7,6},{8,9},{11,10},{12,13},{15,14},{16,17},{19,... | collective-permute-start | bytes 3145736 | tf_op jit(solution)/shard_map/ppermute | solution.py:294
  67.3 12.8 %collective-permute-done.9.refs_2_ = bf16[256,2048]{1,0:T(8,128)(2,1)S(1)} collective-permute-done((bf16[256,2048]{1,0:T(8,128)(2,1)S(1)}, bf16[256,2048]{1,0:T(8,128)(2,1)S(1)}, u32[]{:S(2)}, u32[]{:S(2)}) %collective-permute-start.9) | collective-permute-done | bytes 1048608 | tf_op jit(solution)/shard_map/ppermute | solution.py:294
  92.8 6.4 %collective-permute-start.15 = (bf16[256,2048]{1,0:T(8,128)(2,1)S(1)}, bf16[256,2048]{1,0:T(8,128)(2,1)S(1)}, u32[]{:S(2)}, u32[]{:S(2)}) collective-permute-start(bf16[256,2048]{1,0:T(8,128)(2,1)S(1)} %rotated.19.refs_4_.refs_0_), channel_id=1, source_target_pairs={{0,1},{3,2},{4,5},{7,6},{8,9},{11,10},{12,13},{15,14},{16,17},{19,... | collective-permute-start | bytes 3145736 | tf_op jit(solution)/shard_map/ppermute | solution.py:294
  111.3 5.8 %collective-permute-done.15.refs_2_ = bf16[256,2048]{1,0:T(8,128)(2,1)S(1)} collective-permute-done((bf16[256,2048]{1,0:T(8,128)(2,1)S(1)}, bf16[256,2048]{1,0:T(8,128)(2,1)S(1)}, u32[]{:S(2)}, u32[]{:S(2)}) %collective-permute-start.15) | collective-permute-done | bytes 1048608 | tf_op jit(solution)/shard_map/ppermute | solution.py:294
  122.8 4.0 %added.10.refs_4_.refs_1_ = bf16[2048,512]{1,0:T(8,128)(2,1)} custom-call(bf16[2048,512]{1,0:T(8,128)(2,1)S(1)} %copy-done.6, bf16[2048,512]{1,0:T(8,128)(2,1)} %collective-permute-done.10.refs_1_, bf16[1024,512]{1,0:T(8,128)(2,1)} %chosen.9.refs_2_.refs_1_), custom_call_target="tpu_custom_call" | custom-call | flops 1 | bytes 1 | tf_op jit(solution)/shard_map/added/pallas_call | solution.py:66
  128.2 8.5 %collective-permute-done.8.refs_2_ = bf16[256,3072]{1,0:T(8,128)(2,1)} collective-permute-done((bf16[256,3072]{1,0:T(8,128)(2,1)S(1)}, bf16[256,3072]{1,0:T(8,128)(2,1)}, u32[]{:S(2)}, u32[]{:S(2)}) %collective-permute-start.8) | collective-permute-done | bytes 1572896 | tf_op jit(solution)/shard_map/ppermute | solution.py:121
  138.8 10.5 %collective-permute-start.21 = (bf16[256,2048]{1,0:T(8,128)(2,1)S(1)}, bf16[256,2048]{1,0:T(8,128)(2,1)S(1)}, u32[]{:S(2)}, u32[]{:S(2)}) collective-permute-start(bf16[256,2048]{1,0:T(8,128)(2,1)S(1)} %rotated.21.refs_3_.refs_0_.refs_4_), channel_id=1, source_target_pairs={{0,1},{3,2},{4,5},{7,6},{8,9},{11,10},{12,13},{15,14},{16,17},{19,... | collective-permute-start | bytes 3145736 | tf_op jit(solution)/shard_map/ppermute | solution.py:294
  159.8 12.2 %collective-permute-done.21.refs_2_ = bf16[256,2048]{1,0:T(8,128)(2,1)S(1)} collective-permute-done((bf16[256,2048]{1,0:T(8,128)(2,1)S(1)}, bf16[256,2048]{1,0:T(8,128)(2,1)S(1)}, u32[]{:S(2)}, u32[]{:S(2)}) %collective-permute-start.21) | collective-permute-done | bytes 1048608 | tf_op jit(solution)/shard_map/ppermute | solution.py:294
  177.7 4.0 added.11.refs_4_.refs_1_
  183.8 6.9 %collective-permute-start.23 = (bf16[256,2048]{1,0:T(8,128)(2,1)S(1)}, bf16[256,2048]{1,0:T(8,128)(2,1)}, u32[]{:S(2)}, u32[]{:S(2)}) collective-permute-start(bf16[256,2048]{1,0:T(8,128)(2,1)S(1)} %rotated.23.refs_3_.refs_0_.refs_4_), channel_id=1, source_target_pairs={{0,1},{3,2},{4,5},{7,6},{8,9},{11,10},{12,13},{15,14},{16,17},{19,... | collective-permute-start | bytes 3145736 | tf_op jit(solution)/shard_map/ppermute | solution.py:294
  204.6 6.9 %collective-permute-done.23.refs_2_ = bf16[256,2048]{1,0:T(8,128)(2,1)} collective-permute-done((bf16[256,2048]{1,0:T(8,128)(2,1)S(1)}, bf16[256,2048]{1,0:T(8,128)(2,1)}, u32[]{:S(2)}, u32[]{:S(2)}) %collective-permute-start.23) | collective-permute-done | bytes 1048608 | tf_op jit(solution)/shard_map/ppermute | solution.py:294
  225.4 8.1 %collective-permute-start.27 = (bf16[256,2048]{1,0:T(8,128)(2,1)S(1)}, bf16[256,2048]{1,0:T(8,128)(2,1)S(1)}, u32[]{:S(2)}, u32[]{:S(2)}) collective-permute-start(bf16[256,2048]{1,0:T(8,128)(2,1)S(1)} %rotated.25.refs_3_.refs_0_.refs_4_), channel_id=1, source_target_pairs={{0,1},{3,2},{4,5},{7,6},{8,9},{11,10},{12,13},{15,14},{16,17},{19,... | collective-permute-start | bytes 3145736 | tf_op jit(solution)/shard_map/ppermute | solution.py:294
  234.8 6.8 %collective-permute-done.29.refs_2_ = bf16[2048,512]{1,0:T(8,128)(2,1)} collective-permute-done((bf16[2048,512]{1,0:T(8,128)(2,1)}, bf16[2048,512]{1,0:T(8,128)(2,1)}, u32[]{:S(2)}, u32[]{:S(2)}) %collective-permute-start.29) | collective-permute-done | bytes 2097184 | tf_op jit(solution)/shard_map/ppermute | solution.py:314
  251.1 4.0 products.13
  262.0 4.0 added.13.refs_4_.refs_1_
  267.3 8.6 %collective-permute-done.22.refs_2_ = bf16[256,3072]{1,0:T(8,128)(2,1)} collective-permute-done((bf16[256,3072]{1,0:T(8,128)(2,1)S(1)}, bf16[256,3072]{1,0:T(8,128)(2,1)}, u32[]{:S(2)}, u32[]{:S(2)}) %collective-permute-start.22) | collective-permute-done | bytes 1572896 | tf_op jit(solution)/shard_map/ppermute | solution.py:121
  277.7 8.7 %collective-permute-done.31.refs_2_ = bf16[2048,512]{1,0:T(8,128)(2,1)} collective-permute-done((bf16[2048,512]{1,0:T(8,128)(2,1)S(1)}, bf16[2048,512]{1,0:T(8,128)(2,1)}, u32[]{:S(2)}, u32[]{:S(2)}) %collective-permute-start.31) | collective-permute-done | bytes 2097184 | tf_op jit(solution)/shard_map/ppermute | solution.py:314
  303.6 4.4 %added.14.refs_3_.refs_1_ = bf16[2048,512]{1,0:T(8,128)(2,1)} custom-call(bf16[2048,512]{1,0:T(8,128)(2,1)} %partial_grad.14.refs_2_.refs_0_, bf16[2048,512]{1,0:T(8,128)(2,1)} %collective-permute-done.34.refs_1_, bf16[256,13312]{1,0:T(8,128)(2,1)} %rotated.29.refs_2_.refs_4_), custom_call_target="tpu_custom_call" | custom-call | flops 1 | bytes 1 | tf_op jit(solution)/shard_map/added/pallas_call | solution.py:66
  309.4 22.0 %collective-permute-done.33.refs_2_ = bf16[2048,512]{1,0:T(8,128)(2,1)} collective-permute-done((bf16[2048,512]{1,0:T(8,128)(2,1)}, bf16[2048,512]{1,0:T(8,128)(2,1)}, u32[]{:S(2)}, u32[]{:S(2)}) %collective-permute-start.33) | collective-permute-done | bytes 2097184 | tf_op jit(solution)/shard_map/ppermute | solution.py:314
  342.0 17.9 %collective-permute-done.39.refs_2_ = bf16[256,2048]{1,0:T(8,128)(2,1)S(1)} collective-permute-done((bf16[256,2048]{1,0:T(8,128)(2,1)S(1)}, bf16[256,2048]{1,0:T(8,128)(2,1)S(1)}, u32[]{:S(2)}, u32[]{:S(2)}) %collective-permute-start.39) | collective-permute-done | bytes 1048608 | tf_op jit(solution)/shard_map/ppermute | solution.py:121
  364.2 12.1 %collective-permute-done.41.refs_2_ = bf16[2048,512]{1,0:T(8,128)(2,1)} collective-permute-done((bf16[2048,512]{1,0:T(8,128)(2,1)}, bf16[2048,512]{1,0:T(8,128)(2,1)}, u32[]{:S(2)}, u32[]{:S(2)}) %collective-permute-start.41) | collective-permute-done | bytes 2097184 | tf_op jit(solution)/shard_map/ppermute | solution.py:314
  386.6 10.1 %collective-permute-done.44.refs_2_ = bf16[1024,512]{1,0:T(8,128)(2,1)} collective-permute-done((bf16[1024,512]{1,0:T(8,128)(2,1)S(1)}, bf16[1024,512]{1,0:T(8,128)(2,1)}, u32[]{:S(2)}, u32[]{:S(2)}) %collective-permute-start.44) | collective-permute-done | bytes 1048608 | tf_op jit(solution)/shard_map/ppermute | solution.py:314
  (192 shorter events, 199.7 us)
Async XLA Ops:
  0.6 48.0 %collective-permute-start = (bf16[13312,512]{1,0:T(8,128)(2,1)}, bf16[13312,512]{1,0:T(8,128)(2,1)}, u32[]{:S(2)}, u32[]{:S(2)}) collective-permute-start(bf16[13312,512]{1,0:T(8,128)(2,1)} %refs_2_.15), channel_id=1, source_target_pairs={{0,4},{4,0},{8,12},{12,8},{1,5},{5,1},{9,13},{13,9},{2,6},{6,2},{1... | collective-permute-start | bytes 40894472 | tf_op jit(solution)/shard_map/ppermute | solution.py:121
  51.6 39.1 %collective-permute-start.14 = (bf16[256,3072]{1,0:T(8,128)(2,1)}, bf16[256,3072]{1,0:T(8,128)(2,1)}, u32[]{:S(2)}, u32[]{:S(2)}) collective-permute-start(bf16[256,3072]{1,0:T(8,128)(2,1)} %get-tuple-element.20.refs_4_.refs_1_), channel_id=1, source_target_pairs={{0,8},{4,12},{8,0},{12,4},{1,9},{5,13},{9,1},{13,5},{2,10},{6,14},... | collective-permute-start | bytes 4718600 | tf_op jit(solution)/shard_map/ppermute | solution.py:121
  82.7 40.1 %collective-permute-start.10 = (bf16[2048,512]{1,0:T(8,128)(2,1)}, bf16[2048,512]{1,0:T(8,128)(2,1)}, u32[]{:S(2)}, u32[]{:S(2)}) collective-permute-start(bf16[2048,512]{1,0:T(8,128)(2,1)} %partial_grad.10.refs_3_.refs_0_), channel_id=1, source_target_pairs={{1,2},{2,1},{5,6},{6,5},{9,10},{10,9},{13,14},{14,13},{17,18},{18,... | collective-permute-start | bytes 6291464 | tf_op jit(solution)/shard_map/ppermute | solution.py:307
  99.2 37.5 %collective-permute-start.8 = (bf16[256,3072]{1,0:T(8,128)(2,1)S(1)}, bf16[256,3072]{1,0:T(8,128)(2,1)}, u32[]{:S(2)}, u32[]{:S(2)}) collective-permute-start(bf16[256,3072]{1,0:T(8,128)(2,1)S(1)} %get-tuple-element.21.refs_4_.refs_1_), channel_id=1, source_target_pairs={{0,8},{4,12},{8,0},{12,4},{1,9},{5,13},{9,1},{13,5},{2,10},{6,14},... | collective-permute-start | bytes 4718600 | tf_op jit(solution)/shard_map/ppermute | solution.py:121
  118.9 57.0 %collective-permute-start.20 = (bf16[2048,512]{1,0:T(8,128)(2,1)S(1)}, bf16[2048,512]{1,0:T(8,128)(2,1)}, u32[]{:S(2)}, u32[]{:S(2)}) collective-permute-start(bf16[2048,512]{1,0:T(8,128)(2,1)S(1)} %partial_grad.11.refs_3_.refs_0_), channel_id=1, source_target_pairs={{1,2},{2,1},{5,6},{6,5},{9,10},{10,9},{13,14},{14,13},{17,18},{18,... | collective-permute-start | bytes 6291464 | tf_op jit(solution)/shard_map/ppermute | solution.py:307
  121.0 60.8 %collective-permute-start.17 = (bf16[256,4096]{1,0:T(8,128)(2,1)S(1)}, bf16[256,4096]{1,0:T(8,128)(2,1)}, u32[]{:S(2)}, u32[]{:S(2)}) collective-permute-start(bf16[256,4096]{1,0:T(8,128)(2,1)S(1)} %copy-done.2), channel_id=1, source_target_pairs={{0,8},{4,12},{8,0},{12,4},{1,9},{5,13},{9,1},{13,5},{2,10},{6,14},... | collective-permute-start | bytes 6291464 | tf_op jit(solution)/shard_map/ppermute | solution.py:121
  126.8 63.9 %collective-permute-start.19 = (bf16[2048,512]{1,0:T(8,128)(2,1)}, bf16[2048,512]{1,0:T(8,128)(2,1)}, u32[]{:S(2)}, u32[]{:S(2)}) collective-permute-start(bf16[2048,512]{1,0:T(8,128)(2,1)} %added.10.refs_4_.refs_1_), channel_id=1, source_target_pairs={{1,0},{2,3},{5,4},{6,7},{9,8},{10,11},{13,12},{14,15},{17,16},{18,... | collective-permute-start | bytes 6291464 | tf_op jit(solution)/shard_map/ppermute | solution.py:314
  138.8 33.3 %collective-permute-start.21 = (bf16[256,2048]{1,0:T(8,128)(2,1)S(1)}, bf16[256,2048]{1,0:T(8,128)(2,1)S(1)}, u32[]{:S(2)}, u32[]{:S(2)}) collective-permute-start(bf16[256,2048]{1,0:T(8,128)(2,1)S(1)} %rotated.21.refs_3_.refs_0_.refs_4_), channel_id=1, source_target_pairs={{0,1},{3,2},{4,5},{7,6},{8,9},{11,10},{12,13},{15,14},{16,17},{19,... | collective-permute-start | bytes 3145736 | tf_op jit(solution)/shard_map/ppermute | solution.py:294
  153.3 41.0 %collective-permute-start.18 = (bf16[1024,512]{1,0:T(8,128)(2,1)}, bf16[1024,512]{1,0:T(8,128)(2,1)S(1)}, u32[]{:S(2)}, u32[]{:S(2)}) collective-permute-start(bf16[1024,512]{1,0:T(8,128)(2,1)} %chosen.9.refs_2_.refs_1_), channel_id=1, source_target_pairs={{0,4},{4,0},{8,12},{12,8},{1,5},{5,1},{9,13},{13,9},{2,6},{6,2},{1... | collective-permute-start | bytes 3145736 | tf_op jit(solution)/shard_map/ppermute | solution.py:121
  173.8 43.5 %collective-permute-start.26 = (bf16[2048,512]{1,0:T(8,128)(2,1)S(1)}, bf16[2048,512]{1,0:T(8,128)(2,1)}, u32[]{:S(2)}, u32[]{:S(2)}) collective-permute-start(bf16[2048,512]{1,0:T(8,128)(2,1)S(1)} %partial_grad.12.refs_2_.refs_0_), channel_id=1, source_target_pairs={{1,2},{2,1},{5,6},{6,5},{9,10},{10,9},{13,14},{14,13},{17,18},{18,... | collective-permute-start | bytes 6291464 | tf_op jit(solution)/shard_map/ppermute | solution.py:307
  175.9 47.5 %collective-permute-start.25 = (bf16[256,4096]{1,0:T(8,128)(2,1)S(1)}, bf16[256,4096]{1,0:T(8,128)(2,1)}, u32[]{:S(2)}, u32[]{:S(2)}) collective-permute-start(bf16[256,4096]{1,0:T(8,128)(2,1)S(1)} %copy-done.4), channel_id=1, source_target_pairs={{0,8},{4,12},{8,0},{12,4},{1,9},{5,13},{9,1},{13,5},{2,10},{6,14},... | collective-permute-start | bytes 6291464 | tf_op jit(solution)/shard_map/ppermute | solution.py:121
  190.8 50.8 %collective-permute-start.29 = (bf16[2048,512]{1,0:T(8,128)(2,1)}, bf16[2048,512]{1,0:T(8,128)(2,1)}, u32[]{:S(2)}, u32[]{:S(2)}) collective-permute-start(bf16[2048,512]{1,0:T(8,128)(2,1)} %added.11.refs_4_.refs_1_), channel_id=1, source_target_pairs={{1,0},{2,3},{5,4},{6,7},{9,8},{10,11},{13,12},{14,15},{17,16},{18,... | collective-permute-start | bytes 6291464 | tf_op jit(solution)/shard_map/ppermute | solution.py:314
  194.4 49.9 %collective-permute-start.28 = (bf16[2048,512]{1,0:T(8,128)(2,1)S(1)}, bf16[2048,512]{1,0:T(8,128)(2,1)}, u32[]{:S(2)}, u32[]{:S(2)}) collective-permute-start(bf16[2048,512]{1,0:T(8,128)(2,1)S(1)} %chosen.10.refs_4_.refs_1_), channel_id=1, source_target_pairs={{0,4},{4,0},{8,12},{12,8},{1,5},{5,1},{9,13},{13,9},{2,6},{6,2},{1... | collective-permute-start | bytes 6291464 | tf_op jit(solution)/shard_map/ppermute | solution.py:121
  215.2 46.7 %collective-permute-start.24 = (bf16[2048,512]{1,0:T(8,128)(2,1)}, bf16[2048,512]{1,0:T(8,128)(2,1)}, u32[]{:S(2)}, u32[]{:S(2)}) collective-permute-start(bf16[2048,512]{1,0:T(8,128)(2,1)} %partial_grad.13.refs_2_.refs_0_), channel_id=1, source_target_pairs={{1,2},{2,1},{5,6},{6,5},{9,10},{10,9},{13,14},{14,13},{17,18},{18,... | collective-permute-start | bytes 6291464 | tf_op jit(solution)/shard_map/ppermute | solution.py:307
  233.5 53.0 %collective-permute-start.31 = (bf16[2048,512]{1,0:T(8,128)(2,1)S(1)}, bf16[2048,512]{1,0:T(8,128)(2,1)}, u32[]{:S(2)}, u32[]{:S(2)}) collective-permute-start(bf16[2048,512]{1,0:T(8,128)(2,1)S(1)} %added.12.refs_4_.refs_1_), channel_id=1, source_target_pairs={{1,0},{2,3},{5,4},{6,7},{9,8},{10,11},{13,12},{14,15},{17,16},{18,... | collective-permute-start | bytes 6291464 | tf_op jit(solution)/shard_map/ppermute | solution.py:314
  241.5 34.3 %collective-permute-start.22 = (bf16[256,3072]{1,0:T(8,128)(2,1)S(1)}, bf16[256,3072]{1,0:T(8,128)(2,1)}, u32[]{:S(2)}, u32[]{:S(2)}) collective-permute-start(bf16[256,3072]{1,0:T(8,128)(2,1)S(1)} %get-tuple-element.27.refs_4_.refs_1_), channel_id=1, source_target_pairs={{0,8},{4,12},{8,0},{12,4},{1,9},{5,13},{9,1},{13,5},{2,10},{6,14},... | collective-permute-start | bytes 4718600 | tf_op jit(solution)/shard_map/ppermute | solution.py:121
  244.3 45.5 %collective-permute-start.30 = (bf16[2048,512]{1,0:T(8,128)(2,1)S(1)}, bf16[2048,512]{1,0:T(8,128)(2,1)}, u32[]{:S(2)}, u32[]{:S(2)}) collective-permute-start(bf16[2048,512]{1,0:T(8,128)(2,1)S(1)} %chosen.11.refs_4_.refs_1_), channel_id=1, source_target_pairs={{0,4},{4,0},{8,12},{12,8},{1,5},{5,1},{9,13},{13,9},{2,6},{6,2},{1... | collective-permute-start | bytes 6291464 | tf_op jit(solution)/shard_map/ppermute | solution.py:121
  260.0 43.6 %collective-permute-start.34 = (bf16[2048,512]{1,0:T(8,128)(2,1)}, bf16[2048,512]{1,0:T(8,128)(2,1)}, u32[]{:S(2)}, u32[]{:S(2)}) collective-permute-start(bf16[2048,512]{1,0:T(8,128)(2,1)} %partial_grad.14.refs_2_.refs_0_), channel_id=1, source_target_pairs={{1,2},{2,1},{5,6},{6,5},{9,10},{10,9},{13,14},{14,13},{17,18},{18,... | collective-permute-start | bytes 6291464 | tf_op jit(solution)/shard_map/ppermute | solution.py:307
  266.0 65.4 %collective-permute-start.33 = (bf16[2048,512]{1,0:T(8,128)(2,1)}, bf16[2048,512]{1,0:T(8,128)(2,1)}, u32[]{:S(2)}, u32[]{:S(2)}) collective-permute-start(bf16[2048,512]{1,0:T(8,128)(2,1)} %added.13.refs_4_.refs_1_), channel_id=1, source_target_pairs={{1,0},{2,3},{5,4},{6,7},{9,8},{10,11},{13,12},{14,15},{17,16},{18,... | collective-permute-start | bytes 6291464 | tf_op jit(solution)/shard_map/ppermute | solution.py:314
  289.8 45.3 %collective-permute-start.32 = (bf16[2048,512]{1,0:T(8,128)(2,1)S(1)}, bf16[2048,512]{1,0:T(8,128)(2,1)}, u32[]{:S(2)}, u32[]{:S(2)}) collective-permute-start(bf16[2048,512]{1,0:T(8,128)(2,1)S(1)} %chosen.12.refs_4_.refs_1_), channel_id=1, source_target_pairs={{0,4},{4,0},{8,12},{12,8},{1,5},{5,1},{9,13},{13,9},{2,6},{6,2},{1... | collective-permute-start | bytes 6291464 | tf_op jit(solution)/shard_map/ppermute | solution.py:121
  308.0 68.3 %collective-permute-start.41 = (bf16[2048,512]{1,0:T(8,128)(2,1)}, bf16[2048,512]{1,0:T(8,128)(2,1)}, u32[]{:S(2)}, u32[]{:S(2)}) collective-permute-start(bf16[2048,512]{1,0:T(8,128)(2,1)} %added.14.refs_3_.refs_1_), channel_id=1, source_target_pairs={{1,0},{2,3},{5,4},{6,7},{9,8},{10,11},{13,12},{14,15},{17,16},{18,... | collective-permute-start | bytes 6291464 | tf_op jit(solution)/shard_map/ppermute | solution.py:314
  333.7 45.0 %collective-permute-start.40 = (bf16[2048,512]{1,0:T(8,128)(2,1)S(1)}, bf16[2048,512]{1,0:T(8,128)(2,1)S(1)}, u32[]{:S(2)}, u32[]{:S(2)}) collective-permute-start(bf16[2048,512]{1,0:T(8,128)(2,1)S(1)} %chosen.13.refs_4_.refs_1_), channel_id=1, source_target_pairs={{0,4},{4,0},{8,12},{12,8},{1,5},{5,1},{9,13},{13,9},{2,6},{6,2},{1... | collective-permute-start | bytes 6291464 | tf_op jit(solution)/shard_map/ppermute | solution.py:121
  340.3 41.8 %collective-permute-start.38 = (bf16[256,1024]{1,0:T(8,128)(2,1)S(1)}, bf16[256,1024]{1,0:T(8,128)(2,1)S(1)}, u32[]{:S(2)}, u32[]{:S(2)}) collective-permute-start(bf16[256,1024]{1,0:T(8,128)(2,1)S(1)} %get-tuple-element.34.refs_5_.refs_1_), channel_id=1, source_target_pairs={{0,8},{4,12},{8,0},{12,4},{1,9},{5,13},{9,1},{13,5},{2,10},{6,14},... | collective-permute-start | bytes 1572872 | tf_op jit(solution)/shard_map/ppermute | solution.py:121
  362.8 34.0 %collective-permute-start.44 = (bf16[1024,512]{1,0:T(8,128)(2,1)S(1)}, bf16[1024,512]{1,0:T(8,128)(2,1)}, u32[]{:S(2)}, u32[]{:S(2)}) collective-permute-start(bf16[1024,512]{1,0:T(8,128)(2,1)S(1)} %added.15.refs_3_.refs_1_), channel_id=1, source_target_pairs={{1,0},{2,3},{5,4},{6,7},{9,8},{10,11},{13,12},{14,15},{17,16},{18,... | collective-permute-start | bytes 3145736 | tf_op jit(solution)/shard_map/ppermute | solution.py:314
  (50 other events, 677.6 us)
